TPU v7x, 32 devices: a whole 2x2x4 slice. The times are simulated.
32 devices in a mesh: dp: 4 (over x, core), expert: 8 (over z, y).
Axes of the slice: x: 2, y: 2, z: 4, core: 2. Of those that a mesh axis runs over, the one named last changes fastest.
Arguments:
- tokens: bfloat16 [4096, 2048], P(('dp', 'expert')), may hold values from -6 to 6
- routes: int32 [4096, 2], P(('dp', 'expert')), may hold values from 0 to 15, all different within a row; in each aligned block of 128 rows (0 to 127, 128 to 255, ...) at most 20 rows name the same one
- gate_fixed: int32 [4096, 2], P(('dp', 'expert')), may hold values from 8192 to 57344
- up_weight: bfloat16 [16, 2048, 7168], P('expert', None, 'dp'), may hold values from -0.125 to 0.125
- up_mask: int32 [16, 16, 56], P('expert', None, 'dp'), may hold values 0 or 1
- down_weight: bfloat16 [16, 7168, 2048], P('expert', 'dp'), may hold values from -0.0625 to 0.0625
- down_mask: int32 [16, 56, 16], P('expert', 'dp'), may hold values 0 or 1
- threshold: int32 [16, 7168], P('expert', 'dp'), may hold values from 1 to 8
- cotangent: bfloat16 [4096, 2048], P('dp', 'expert'), may hold values from -6 to 6
Outputs:
- mixed: bfloat16 [4096, 2048], P('dp', 'expert')
- gate_grad: float32 [4096, 2], P(('dp', 'expert'))
- potential_grad: bfloat16 [640, 16, 7168], P(None, 'expert', 'dp')
Inputs may be any that keep to these rules, and one draw needn't show every extreme that they name: In each aligned block of 128 rows, no expert is named by more than 20 rows, a bound that some block reaches; the two routes of a token differ.
All inputs are finite; a program needn't handle non-finite values. No bound on the sum of `up_mask` or of `down_mask` on one device may be relied on, other than what follows from the above.
Results may differ from a plain program's by a relative error of at most 0.02.
Values may be sent and summed in bfloat16 or wider, within the bound.
A program may use at most 192 MiB of HBM per device.

v0:
```python
import math

import jax
import jax.numpy as jnp
from jax import lax
from jax.sharding import PartitionSpec as P

BLOCK = 128


def widen_mask(mask, side):
    return jnp.repeat(jnp.repeat(mask, side, axis=1), side, axis=2).astype(jnp.bfloat16)


def slot_numbers(flat_routes, experts):
    onehot = (flat_routes[..., None] == jnp.arange(experts, dtype=jnp.int32)).astype(jnp.int32)
    earlier = jnp.cumsum(onehot, axis=-2) - onehot
    return jnp.sum(onehot * earlier, axis=-1)


def fill_table(place, count):
    return (
        jnp.full((count,), -1, jnp.int32).at[place].set(jnp.arange(place.shape[0], dtype=jnp.int32))
    )


def take_rows(values, table, per):
    picked = values[jnp.maximum(table, 0) // per]
    return jnp.where((table >= 0)[:, None], picked, jnp.zeros_like(picked))


def shards(
    tokens, routes, gate_fixed, up_weight, up_mask, down_weight, down_mask, threshold, cotangent
):
    owners = lax.axis_size("expert")
    replicas = lax.axis_size("dp")
    tok_rows = tokens.shape[0]
    width = tokens.shape[1]
    local_experts = up_weight.shape[0]
    experts = local_experts * owners
    capacity = (tok_rows * 5 + 2 * experts - 1) // (2 * experts)
    inv_root = 1.0 / math.sqrt(width)
    flat = routes.reshape(-1)
    slot = slot_numbers(flat, experts)
    place = (flat // local_experts * capacity + slot) * local_experts + flat % local_experts
    table = fill_table(place, owners * capacity * local_experts)
    send_rows = take_rows(tokens, table, 2).reshape(owners, capacity, local_experts, width)
    w_up = up_weight * widen_mask(up_mask, BLOCK)
    w_down = down_weight * widen_mask(down_mask, BLOCK)
    scale = 4.0 / threshold.astype(jnp.float32)
    copies = jnp.broadcast_to(send_rows[None], (replicas,) + send_rows.shape)
    copies = copies.reshape(replicas * owners, capacity, local_experts, width)
    arrived = lax.all_to_all(copies, ("dp", "expert"), split_axis=0, concat_axis=0, tiled=True)
    potential = jnp.einsum(
        "red,edf->ref",
        arrived.reshape(-1, local_experts, width),
        w_up,
        preferred_element_type=jnp.float32,
    )
    sig = jax.nn.sigmoid(potential)
    activate_hidden = (potential * sig * scale[None]).astype(jnp.bfloat16)
    activate_slope = (sig * (1.0 + potential * (1.0 - sig)) * scale[None]).astype(jnp.bfloat16)
    both = jnp.stack((activate_hidden, activate_slope), axis=1)
    hidden = both[:, 0]
    slope = both[:, 1]
    part = hidden
    summed = lax.psum_scatter(
        jnp.einsum("ref,efd->red", part, w_down, preferred_element_type=jnp.float32).astype(
            jnp.bfloat16
        ),
        "dp",
        scatter_dimension=0,
        tiled=True,
    )
    gates = gate_fixed.astype(jnp.float32) / 65536.0
    back_rows = lax.all_to_all(
        summed.reshape(owners, capacity, local_experts, width),
        "expert",
        split_axis=0,
        concat_axis=0,
        tiled=True,
    )
    picked = back_rows.reshape(-1, width)[place].reshape(tok_rows, 2, width)
    combined = jnp.sum(gates[:, :, None] * picked.astype(jnp.float32), axis=1).astype(jnp.bfloat16)
    mixed = lax.all_to_all(combined, "expert", split_axis=1, concat_axis=0, tiled=True)
    cot_tokens = lax.all_to_all(cotangent, "expert", split_axis=0, concat_axis=1, tiled=True)
    gate_grad = (
        jnp.einsum("td,tkd->tk", cot_tokens, picked, preferred_element_type=jnp.float32) * inv_root
    )
    scaled = (
        (gates[:, :, None] * cot_tokens[:, None, :].astype(jnp.float32))
        .astype(jnp.bfloat16)
        .reshape(-1, width)
    )
    cot_send = take_rows(scaled, table, 1).reshape(owners, capacity, local_experts, width)
    cot_copies = jnp.broadcast_to(cot_send[None], (replicas,) + cot_send.shape)
    cot_copies = cot_copies.reshape(replicas * owners, capacity, local_experts, width)
    cot_arrived = lax.all_to_all(
        cot_copies, ("dp", "expert"), split_axis=0, concat_axis=0, tiled=True
    )
    back = jnp.einsum(
        "red,efd->ref",
        cot_arrived.reshape(-1, local_experts, width),
        w_down,
        preferred_element_type=jnp.float32,
    )
    part = slope
    potential_grad = (back * part.astype(jnp.float32)).astype(jnp.bfloat16)
    return (mixed, gate_grad, potential_grad)


def solution(mesh):
    placed = (
        P(("dp", "expert"), None),
        P(("dp", "expert"), None),
        P(("dp", "expert"), None),
        P("expert", None, "dp"),
        P("expert", None, "dp"),
        P("expert", "dp", None),
        P("expert", "dp", None),
        P("expert", "dp"),
        P("dp", "expert"),
    )
    return jax.shard_map(
        shards,
        mesh=mesh,
        in_specs=placed,
        out_specs=(P("dp", "expert"), P(("dp", "expert"), None), P(None, "expert", "dp")),
        check_vma=False,
    )
```

profile of v0, /device:TPU:0, one launch (start us, length us, event | category | flops | bytes accessed | tf_op | source)
XLA Modules:
  0.0 549.6 jit_solution(3156681090553130259)
XLA Ops:
  7.2 7.4 %all-to-all-start.3 = ((bf16[8,128,256]{2,1,0:T(8,128)(2,1)}), bf16[8,128,256]{2,1,0:T(8,128)(2,1)S(1)}, u32[]{:S(2)}, u32[]{:S(2)}) async-start(bf16[8,128,256]{2,1,0:T(8,128)(2,1)} %bitcast.89), calls=%async_computation.3 | async-start | bytes 1048576 | tf_op jit(solution)/shard_map/all_to_all | solution.py:86
  22.4 3.1 gather.14
  25.4 3.6 all-to-all-done.3
  34.5 3.7 mul.107
  43.0 4.0 gather.17
  47.0 4.5 broadcast_select_fusion
  51.5 4.9 broadcast_in_dim.62
  56.5 3.8 all-to-all-start
  60.5 19.1 %copy.59 = bf16[2,2048,1792]{1,2,0:T(8,128)(2,1)} copy(bf16[2,2048,1792]{2,1,0:T(8,128)(2,1)} %param.12) | data formatting | bytes 29360128 | tf_op args[3]
  80.0 9.9 %broadcast_in_dim.55 = bf16[2,1792,16,128]{3,2,1,0:T(8,128)(2,1)} broadcast(bf16[2,1792,16]{2,1,0:T(8,128)(2,1)S(1)} %bitcast.86), dimensions={0,1,2} | broadcast | bytes 14794752 | tf_op jit(solution)/shard_map/broadcast_in_dim | solution.py:12
  90.0 22.3 %convert_element_type.78 = bf16[2,1792,2048]{2,1,0:T(8,128)(2,1)} reshape(bf16[2,1792,16,128]{3,2,1,0:T(8,128)(2,1)} %broadcast_in_dim.55) | data formatting | bytes 29360128 | tf_op jit(solution)/shard_map/convert_element_type | solution.py:12
  112.3 13.2 %bitcast_multiply_fusion = bf16[2,2048,1792]{1,2,0:T(8,128)(2,1)} fusion(bf16[2,2048,1792]{1,2,0:T(8,128)(2,1)} %copy.59, bf16[2,2048,14]{1,2,0:T(8,128)(2,1)S(1)} %copy.58), kind=kLoop, calls=%fused_computation.4 | loop fusion | flops 7340032 | bytes 29474816 | tf_op jit(solution)/shard_map/mul | solution.py:48
  125.5 54.0 %all-to-all-done = bf16[32,20,2,2048]{3,2,1,0:T(2,128)(2,1)} async-done(((bf16[32,20,2,2048]{3,2,1,0:T(2,128)(2,1)}), bf16[32,20,2,2048]{3,2,1,0:T(2,128)(2,1)}, u32[]{:S(2)}, u32[]{:S(2)}) %all-to-all-start) | async-done | bytes 5242912 | tf_op jit(solution)/shard_map/all_to_all | solution.py:53
  179.5 19.9 %fusion.15 = f32[2,1792,640]{2,1,0:T(8,128)} fusion(bf16[2,2048,1792]{1,2,0:T(8,128)(2,1)} %bitcast_multiply_fusion, bf16[640,2,2048]{2,1,0:T(2,128)(2,1)} %bitcast.7), kind=kOutput, calls=%fused_computation.24 | convolution fusion | flops 9395240960 | bytes 29097984 | tf_op jit(solution)/shard_map/red,edf->ref/dot_general | solution.py:54
  199.4 19.4 %convert_bitcast_fusion = bf16[640,2,2048]{0,2,1:T(8,128)(2,1)} fusion(f32[2,1792,640]{2,1,0:T(8,128)} %fusion.15, f32[2,1792]{1,0:T(2,128)S(1)} %convert_divide_fusion, bf16[2,1792,2048]{2,1,0:T(8,128)(2,1)} %param.14, bf16[2,1792,2048]{2,1,0:T(8,128)(2,1)S(1)} %copy-done.2), kind=kOutput, calls=%fused_computation.26 | convolution fusion | flops 9418964992 | bytes 43792384 | tf_op jit(solution)/shard_map/ref,efd->red/dot_general | solution.py:68
  218.8 13.9 %copy.67 = bf16[640,2,2048]{2,1,0:T(2,128)(2,1)} copy(bf16[640,2,2048]{0,2,1:T(8,128)(2,1)} %convert_bitcast_fusion) | data formatting | bytes 10485760 | tf_op jit(solution)/shard_map/convert_element_type | solution.py:68
  234.6 97.4 %all-reduce.3.cloned.1.call-done = bf16[640,2,2048]{2,1,0:T(2,128)(2,1)} async-done(((bf16[640,2,2048]{2,1,0:T(2,128)(2,1)}), bf16[640,2,2048]{2,1,0:T(2,128)(2,1)}) %all-reduce.3.cloned.1.call-update) | async-done | bytes 5242896
  334.3 36.6 %all_to_all.50 = bf16[8,20,2,2048]{3,2,1,0:T(2,128)(2,1)S(1)} all-to-all(bf16[8,20,2,2048]{3,2,1,0:T(2,128)(2,1)S(1)} %bitcast.85), channel_id=1, replica_groups=mesh['dp'=4,'expert'=8] {'expert'}, dimensions={0} | all-to-all | bytes 2621440 | tf_op jit(solution)/shard_map/all_to_all | solution.py:76
  370.8 4.9 broadcast_in_dim.64
  375.8 3.8 all-to-all-start.4
  388.3 110.2 %all-to-all-done.4 = bf16[32,20,2,2048]{3,2,1,0:T(2,128)(2,1)} async-done(((bf16[32,20,2,2048]{3,2,1,0:T(2,128)(2,1)}), bf16[32,20,2,2048]{3,2,1,0:T(2,128)(2,1)}, u32[]{:S(2)}, u32[]{:S(2)}) %all-to-all-start.4) | async-done | bytes 5242912 | tf_op jit(solution)/shard_map/all_to_all | solution.py:98
  498.5 3.5 all-to-all-start.2
  502.1 24.1 %fusion = bf16[640,2,1792]{0,2,1:T(8,128)(2,1)} fusion(f32[2,1792,640]{2,1,0:T(8,128)} %fusion.15, f32[2,1792]{1,0:T(2,128)S(1)} %convert_divide_fusion, bf16[640,2,2048]{2,1,0:T(2,128)(2,1)} %bitcast.18, bf16[2,1792,2048]{2,1,0:T(8,128)(2,1)} %param.14, bf16[2,1792,2048]{2,1,0:T(8,128)(2,1)} %convert_element_type.78), kind=kOutput, calls=%fused_computation.6 | convolution fusion | flops 9430106112 | bytes 48379904 | tf_op jit(solution)/shard_map/red,efd->ref/dot_general | solution.py:101
  526.2 13.8 %copy.74 = bf16[640,2,1792]{2,1,0:T(2,128)(2,1)} copy(bf16[640,2,1792]{0,2,1:T(8,128)(2,1)} %fusion) | data formatting | bytes 9175040
  (70 shorter events, 33.4 us)
Async XLA Ops:
  7.2 12.2 %copy-start = (bf16[128,2048]{1,0:T(8,128)(2,1)S(1)}, bf16[128,2048]{1,0:T(8,128)(2,1)}, u32[]{:S(2)}) copy-start(bf16[128,2048]{1,0:T(8,128)(2,1)} %param.9) | copy-start | bytes 1572868
  7.2 21.9 %all-to-all-start.3 = ((bf16[8,128,256]{2,1,0:T(8,128)(2,1)}), bf16[8,128,256]{2,1,0:T(8,128)(2,1)S(1)}, u32[]{:S(2)}, u32[]{:S(2)}) async-start(bf16[8,128,256]{2,1,0:T(8,128)(2,1)} %bitcast.89), calls=%async_computation.3 | async-start | bytes 1048576 | tf_op jit(solution)/shard_map/all_to_all | solution.py:86
  32.0 2.5 copy-start.3
  56.5 123.0 %all-to-all-start = ((bf16[32,20,2,2048]{3,2,1,0:T(2,128)(2,1)}), bf16[32,20,2,2048]{3,2,1,0:T(2,128)(2,1)}, u32[]{:S(2)}, u32[]{:S(2)}) async-start(bf16[32,20,2,2048]{3,2,1,0:T(2,128)(2,1)} %bitcast.83), calls=%async_computation | async-start | bytes 10485760 | tf_op jit(solution)/shard_map/all_to_all | solution.py:53
  60.2 19.4 %copy-start.7 = (s32[2,16,14]{1,0,2:T(2,128)S(1)}, s32[2,16,14]{1,0,2:T(2,128)}, u32[]{:S(2)}) copy-start(s32[2,16,14]{1,0,2:T(2,128)} %param.13) | copy-start | bytes 5380
  60.3 19.6 %copy-start.8 = (s32[2,14,16]{2,0,1:T(2,128)S(1)}, s32[2,14,16]{2,0,1:T(2,128)}, u32[]{:S(2)}) copy-start(s32[2,14,16]{2,0,1:T(2,128)} %param.15) | copy-start | bytes 5380
  60.3 271.8 %all-reduce.3.cloned.1.call-start = ((), (), s32[]{:S(2)}) async-start(), calls=%async_computation.5 | async-start | bytes 10485760
  112.3 13.2 %copy-start.6 = (s32[2,1792]{1,0:T(2,128)S(1)}, s32[2,1792]{1,0:T(2,128)}, u32[]{:S(2)}) copy-start(s32[2,1792]{1,0:T(2,128)} %param.16) | copy-start | bytes 43012
  179.5 19.9 %copy-start.2 = (bf16[2,1792,2048]{2,1,0:T(8,128)(2,1)S(1)}, bf16[2,1792,2048]{2,1,0:T(8,128)(2,1)}, u32[]{:S(2)}) copy-start(bf16[2,1792,2048]{2,1,0:T(8,128)(2,1)} %convert_element_type.78) | copy-start | bytes 44040196
  232.7 0.7 copy-start.9
  232.7 138.1 %copy-start.5 = (bf16[8,20,2,2048]{3,2,1,0:T(2,128)(2,1)S(1)}, bf16[8,20,2,2048]{3,2,1,0:T(2,128)(2,1)}, u32[]{:S(2)}) copy-start(bf16[8,20,2,2048]{3,2,1,0:T(2,128)(2,1)} %get-tuple-element.15) | copy-start | bytes 3932164
  375.8 122.8 %all-to-all-start.4 = ((bf16[32,20,2,2048]{3,2,1,0:T(2,128)(2,1)}), bf16[32,20,2,2048]{3,2,1,0:T(2,128)(2,1)}, u32[]{:S(2)}, u32[]{:S(2)}) async-start(bf16[32,20,2,2048]{3,2,1,0:T(2,128)(2,1)} %bitcast.84), calls=%async_computation.4 | async-start | bytes 10485760 | tf_op jit(solution)/shard_map/all_to_all | solution.py:98
  498.5 43.2 %all-to-all-start.2 = ((bf16[128,8,256]{0,2,1:T(8,128)(2,1)}), bf16[128,8,256]{0,2,1:T(8,128)(2,1)S(1)}, u32[]{:S(2)}, u32[]{:S(2)}) async-start(bf16[128,8,256]{0,2,1:T(8,128)(2,1)} %bitcast.11), calls=%async_computation.2 | async-start | bytes 1048576 | tf_op jit(solution)/shard_map/all_to_all | solution.py:85
  502.0 40.7 %copy-start.1 = (bf16[128,2048]{1,0:T(8,128)(2,1)S(1)}, bf16[128,2048]{1,0:T(8,128)(2,1)}, u32[]{:S(2)}) copy-start(bf16[128,2048]{1,0:T(8,128)(2,1)} %param.9) | copy-start | bytes 1572868
  526.2 13.8 %copy-start.4 = (f32[128,2048]{1,0:T(8,128)S(1)}, f32[128,2048]{1,0:T(8,128)}, u32[]{:S(2)}) copy-start(f32[128,2048]{1,0:T(8,128)} %copy-done.3) | copy-start | bytes 3145732
Sparse Core Ops, SparseCore 0:
  232.8 99.1 all-reduce.2
where the time goes:
time: 552 us; the launch traced here: 550 us
  waiting for transfers between devices  265 us (48%)
  local copies, waits for them, and re-layouts  124 us (22%)
  matrix products  63.5 us (12%)
  blocking collectives  36.6 us (7%)
  other arithmetic  26.8 us (5%)
  starting transfers between devices  18.7 us (3%)
  between operations  15 us (3%)
    all_to_all x1, waiting for transfers between devices, shards(): lax.all_to_all(cot_copies, ('dp', 'expert'), split_axis=0, concat_axis=0,...  110 us
    unnamed x2, waiting for transfers between devices  97.5 us
    all_to_all x1, waiting for transfers between devices, shards(): lax.all_to_all(copies, ('dp', 'expert'), split_axis=0, concat_axis=0, til...  54 us
    unnamed x26, local copies, waits for them, and re-layouts  38.7 us
    all_to_all x1, blocking collectives, shards(): lax.all_to_all(summed.reshape(owners, capacity, local_experts, width), 'e...  36.6 us
    dot_general x1, matrix products, shards(): jnp.einsum('red,efd->ref', cot_arrived.reshape(-1, local_experts, width),...  24.1 us
    convert_element_type x4, local copies, waits for them, and re-layouts, widen_mask(): jnp.repeat(jnp.repeat(mask, side, axis=1), side, axis=2)  22.4 us
    dot_general x1, matrix products, shards(): jnp.einsum('red,edf->ref', arrived.reshape(-1, local_experts, width), w_u...  19.9 us
  transfers between devices with their start and end apart: 5, of which 4 were waited for; matrix products, arithmetic and copies ran while one was open for 23% of the time, Pallas kernels for 0%

commit v1 on v0

v1 whole, which is shorter than its diff:
```python
import functools
import math

import jax
import jax.numpy as jnp
from jax import lax
from jax.experimental import pallas as pl
from jax.experimental.pallas import tpu as pltpu
from jax.sharding import PartitionSpec as P

BLOCK = 128
CORES = 2
VMEM_LIMIT = 60 * 1024 * 1024
MESH = pl.DeviceIdType.MESH


def greet(owners, groups):
    me, mine = lax.axis_index("dp"), lax.axis_index("expert")
    turns = groups // CORES
    x, core = me // CORES, me % CORES
    barrier = pltpu.get_barrier_semaphore()

    def hail(k, carry):
        peer = lax.rem(mine + k, owners)
        pl.semaphore_signal(
            barrier, inc=1, device_id={"dp": me, "expert": peer}, device_id_type=MESH
        )
        return carry

    lax.fori_loop(1, owners, hail, 0)
    others = [x * CORES + 1 - core]
    others += [lax.rem(x + d, turns) * CORES + core for d in range(1, turns)]
    for other in others:
        pl.semaphore_signal(
            barrier, inc=1, device_id={"dp": other, "expert": mine}, device_id_type=MESH
        )
    pl.semaphore_wait(barrier, owners - 1 + len(others))


def dispatch_kernel(
    owners, groups, rows_in, cot_in, rows_out, cot_out, local, first, twin, across, landed
):
    me, mine = lax.axis_index("dp"), lax.axis_index("expert")
    turns = groups // CORES
    x, core = me // CORES, me % CORES
    other_core = x * CORES + 1 - core
    height, breadth = cot_in.shape[2], cot_in.shape[3]
    ins = (rows_in, cot_in)

    def spot(kind, group, source):
        if kind == 0:
            return rows_out.at[group * owners + source]
        top = pl.multiple_of(group * height, 16)
        return cot_out.at[
            :, pl.ds(top, height), pl.ds(pl.multiple_of(source * breadth, 128), breadth)
        ]

    def send_first(kind, k):
        peer = lax.rem(mine + k, owners)
        return pltpu.make_async_remote_copy(
            src_ref=ins[kind].at[peer],
            dst_ref=spot(kind, me, mine),
            send_sem=first.at[kind, k],
            recv_sem=landed.at[kind, me, mine],
            device_id={"dp": me, "expert": peer},
            device_id_type=MESH,
        )

    def keep(kind):
        return pltpu.make_async_copy(ins[kind].at[mine], spot(kind, me, mine), local.at[kind])

    def relay(kind, d, source):
        group = lax.rem(x + turns - d, turns) * CORES + core
        return pltpu.make_async_remote_copy(
            src_ref=spot(kind, group, source),
            dst_ref=spot(kind, group, source),
            send_sem=twin.at[kind, d, source],
            recv_sem=landed.at[kind, group, source],
            device_id={"dp": other_core, "expert": mine},
            device_id_type=MESH,
        )

    def cross(kind, d, source):
        return pltpu.make_async_remote_copy(
            src_ref=spot(kind, me, source),
            dst_ref=spot(kind, me, source),
            send_sem=across.at[kind, d, source],
            recv_sem=landed.at[kind, me, source],
            device_id={"dp": lax.rem(x + d, turns) * CORES + core, "expert": mine},
            device_id_type=MESH,
        )

    def arrival(kind, group, source):
        return pltpu.make_async_remote_copy(
            src_ref=spot(kind, group, source),
            dst_ref=spot(kind, group, source),
            send_sem=first.at[kind, 0],
            recv_sem=landed.at[kind, group, source],
            device_id={"dp": other_core, "expert": mine},
            device_id_type=MESH,
        )

    def over(low, body):
        def step(k, carry):
            body(k)
            return carry

        lax.fori_loop(low, owners, step, 0)

    greet(owners, groups)
    for kind in (0, 1):
        keep(kind).start()
        over(1, lambda k: send_first(kind, k).start())

    def pass_on(kind, source):
        for d in range(1, turns):
            cross(kind, d, source).start()
        relay(kind, 0, source).start()

    for kind in (0, 1):
        keep(kind).wait()
        pass_on(kind, mine)

        def own(k):
            source = lax.rem(mine + owners - k, owners)
            arrival(kind, me, source).wait_recv()
            pass_on(kind, source)

        over(1, own)
        for d in range(1, turns):
            group = lax.rem(x + turns - d, turns) * CORES + core

            def far(k):
                source = lax.rem(mine + owners - k, owners)
                arrival(kind, group, source).wait_recv()
                relay(kind, d, source).start()

            over(0, far)
    for kind in (0, 1):
        for d in range(turns):
            group = lax.rem(x + turns - d, turns) * CORES + 1 - core
            over(0, lambda k: arrival(kind, group, k).wait_recv())
        over(1, lambda k: send_first(kind, k).wait_send())
        for d in range(turns):
            over(0, lambda k: relay(kind, d, k).wait_send())
        for d in range(1, turns):
            over(0, lambda k: cross(kind, d, k).wait_send())


def dispatch(rows_in, cot_in, owners, groups):
    _, packed, piece = rows_in.shape
    _, experts, height, breadth = cot_in.shape
    turns = groups // CORES
    return pl.pallas_call(
        functools.partial(dispatch_kernel, owners, groups),
        out_shape=(
            jax.ShapeDtypeStruct((groups * owners, packed, piece), jnp.bfloat16),
            jax.ShapeDtypeStruct((experts, groups * height, owners * breadth), jnp.bfloat16),
        ),
        in_specs=[pl.BlockSpec(memory_space=pl.ANY)] * 2,
        out_specs=(pl.BlockSpec(memory_space=pl.ANY),) * 2,
        scratch_shapes=[
            pltpu.SemaphoreType.DMA((2,)),
            pltpu.SemaphoreType.DMA((2, owners)),
            pltpu.SemaphoreType.DMA((2, turns, owners)),
            pltpu.SemaphoreType.DMA((2, turns, owners)),
            pltpu.SemaphoreType.DMA((2, groups, owners)),
        ],
        compiler_params=pltpu.CompilerParams(
            collective_id=0, has_side_effects=True, vmem_limit_bytes=VMEM_LIMIT
        ),
        name="dispatch",
    )(rows_in, cot_in)


def return_kernel(
    owners, groups, halves, part, ret, near, sums, far, done,
    near_s, near_r, far_s, far_r, back_s, back_r, local
):
    me, mine = lax.axis_index("dp"), lax.axis_index("expert")
    turns = groups // CORES
    x, core = me // CORES, me % CORES
    other_core = x * CORES + 1 - core
    experts, _, height, width = part.shape
    rows = height // halves
    breadth = width // owners
    chunks = [(e, h) for e in range(experts) for h in range(halves)]
    order = list(range(1, turns)) + [0]

    def band(h):
        return pl.ds(h * rows, rows)

    def fold(e, h, d):
        group = lax.rem(x + d, turns) * CORES + 1 - core
        return pltpu.make_async_remote_copy(
            src_ref=part.at[e, group, band(h)],
            dst_ref=near.at[e, d, band(h)],
            send_sem=near_s.at[e, h, d],
            recv_sem=near_r.at[e, h, d],
            device_id={"dp": other_core, "expert": mine},
            device_id_type=MESH,
        )

    def cross(e, h, d):
        return pltpu.make_async_remote_copy(
            src_ref=sums.at[e, d, band(h)],
            dst_ref=far.at[e, d - 1, band(h)],
            send_sem=far_s.at[e, h, d],
            recv_sem=far_r.at[e, h, d],
            device_id={"dp": lax.rem(x + d, turns) * CORES + core, "expert": mine},
            device_id_type=MESH,
        )

    def columns(owner):
        return pl.ds(pl.multiple_of(owner * breadth, 128), breadth)

    def give(e, h, k):
        peer = lax.rem(mine + k, owners)
        return pltpu.make_async_remote_copy(
            src_ref=done.at[e, band(h), columns(peer)],
            dst_ref=ret.at[mine, e, band(h)],
            send_sem=back_s.at[e, h, k],
            recv_sem=back_r.at[e, h, mine],
            device_id={"dp": me, "expert": peer},
            device_id_type=MESH,
        )

    def keep(e, h):
        return pltpu.make_async_copy(
            done.at[e, band(h), columns(mine)], ret.at[mine, e, band(h)], local.at[e, h]
        )

    def arrival(e, h, source):
        return pltpu.make_async_remote_copy(
            src_ref=done.at[e, band(h), columns(source)],
            dst_ref=ret.at[source, e, band(h)],
            send_sem=back_s.at[e, h, 0],
            recv_sem=back_r.at[e, h, source],
            device_id={"dp": other_core, "expert": mine},
            device_id_type=MESH,
        )

    def over(body):
        def step(k, carry):
            body(k)
            return carry

        lax.fori_loop(1, owners, step, 0)

    greet(owners, groups)
    for e, h in chunks:
        for d in order:
            fold(e, h, d).start()
    for e, h in chunks:
        for d in order:
            fold(e, h, d).wait_recv()
            group = lax.rem(x + d, turns) * CORES + core
            sums[e, d, band(h)] = (
                part[e, group, band(h)].astype(jnp.float32)
                + near[e, d, band(h)].astype(jnp.float32)
            ).astype(jnp.bfloat16)
            if d > 0:
                cross(e, h, d).start()
    for e, h in chunks:
        total = sums[e, 0, band(h)].astype(jnp.float32)
        for d in range(1, turns):
            cross(e, h, d).wait_recv()
            total = total + far[e, d - 1, band(h)].astype(jnp.float32)
        done[e, band(h)] = total.astype(jnp.bfloat16)
        over(lambda k: give(e, h, k).start())
        keep(e, h).start()
    for e, h in chunks:
        keep(e, h).wait()
        over(lambda k: arrival(e, h, lax.rem(mine + k, owners)).wait_recv())
        over(lambda k: give(e, h, k).wait_send())
        for d in range(turns):
            fold(e, h, d).wait_send()
        for d in range(1, turns):
            cross(e, h, d).wait_send()


def reduce_return(part, owners):
    experts, groups, height, width = part.shape
    turns = groups // CORES
    halves = 2 if height % 32 == 0 else 1
    sems = pltpu.SemaphoreType.DMA
    return pl.pallas_call(
        functools.partial(return_kernel, owners, groups, halves),
        out_shape=jax.ShapeDtypeStruct((owners, experts, height, width // owners), jnp.bfloat16),
        in_specs=[pl.BlockSpec(memory_space=pltpu.VMEM)],
        out_specs=pl.BlockSpec(memory_space=pl.ANY),
        scratch_shapes=[
            pltpu.VMEM((experts, turns, height, width), jnp.bfloat16),
            pltpu.VMEM((experts, turns, height, width), jnp.bfloat16),
            pltpu.VMEM((experts, max(1, turns - 1), height, width), jnp.bfloat16),
            pltpu.VMEM((experts, height, width), jnp.bfloat16),
            sems((experts, halves, turns)),
            sems((experts, halves, turns)),
            sems((experts, halves, turns)),
            sems((experts, halves, turns)),
            sems((experts, halves, owners)),
            sems((experts, halves, owners)),
            sems((experts, halves)),
        ],
        compiler_params=pltpu.CompilerParams(
            collective_id=1, has_side_effects=True, vmem_limit_bytes=VMEM_LIMIT
        ),
        name="reduce_return",
    )(part)


def masked(weights, mask):
    return (weights.reshape(mask.shape[0], BLOCK, -1) * mask[:, None, :]).reshape(weights.shape)


def forward_kernel(
    span, arrived, pick, w_up, m_up, w_down, m_down, scale, part, slope, rows, total
):
    tile, tiles = pl.program_id(1), pl.num_programs(1)
    pieces, out_rows = pick.shape[1], pick.shape[2]
    piece = arrived.shape[2]

    @pl.when(tile == 0)
    def _():
        def unpack(g, carry):
            box = arrived[pl.ds(g * span, span)].reshape(-1, piece)
            for q in range(pieces):
                rows[pl.ds(pl.multiple_of(g * out_rows, 16), out_rows), q * piece:(q + 1) * piece] = jnp.dot(
                    pick[0, q], box, preferred_element_type=jnp.float32
                ).astype(jnp.bfloat16)
            return carry

        lax.fori_loop(0, arrived.shape[0] // span, unpack, 0)

    up = masked(w_up[0], m_up[0])
    potential = jnp.dot(rows[...], up, preferred_element_type=jnp.float32)
    sig = jax.nn.sigmoid(potential)
    scaled = sig * scale[0]
    hidden = (potential * scaled).astype(jnp.bfloat16)
    slope[0] = (scaled * (1.0 + potential * (1.0 - sig))).astype(jnp.bfloat16)
    down = masked(w_down[0], m_down[0, 0])
    term = jnp.dot(hidden, down, preferred_element_type=jnp.float32)

    @pl.when(tile == 0)
    def _():
        total[...] = term

    @pl.when(tile > 0)
    def _():
        total[...] += term

    @pl.when(tile == tiles - 1)
    def _():
        part[0] = total[...].astype(jnp.bfloat16)


def backward_kernel(grad, w_down, m_down, slope, out):
    down = masked(w_down[0], m_down[0, 0])
    back = lax.dot_general(
        grad[0], down, (((1,), (1,)), ((), ())), preferred_element_type=jnp.float32
    )
    out[...] = (back * slope[0].astype(jnp.float32)).astype(jnp.bfloat16)


def places(routes, experts, capacity):
    onehot = (routes[..., None] == jnp.arange(experts, dtype=jnp.int32)).astype(jnp.bfloat16)
    count = routes.shape[1]
    at = jnp.arange(count)
    earlier = jnp.einsum(
        "ab,nbe->nae",
        (at[:, None] > at[None, :]).astype(jnp.bfloat16),
        onehot,
        preferred_element_type=jnp.float32,
    )
    slot = jnp.sum(earlier * onehot.astype(jnp.float32), axis=-1).astype(jnp.int32)
    place = routes * capacity + slot
    return (place[..., None] == jnp.arange(experts * capacity, dtype=jnp.int32)).astype(jnp.bfloat16)


def shards(
    tokens, routes, gate_fixed, up_weight, up_mask, down_weight, down_mask, threshold, cotangent
):
    owners = lax.axis_size("expert")
    groups = lax.axis_size("dp")
    tok_rows, width = tokens.shape
    held, _, hidden = up_weight.shape
    experts = held * owners
    capacity = (tok_rows * 5 + 2 * experts - 1) // (2 * experts)
    blocks = owners * groups
    all_rows = blocks * capacity
    height = owners * capacity
    breadth = width // owners
    pieces = 1
    while (held * capacity * pieces) % 16:
        pieces *= 2
    piece = width // pieces
    span = 1
    while (span * capacity) % 16:
        span *= 2
    tile = 256 if hidden % 256 == 0 else BLOCK
    tiles = hidden // tile

    own = places(routes.reshape(1, -1), experts, capacity)[0]
    choose = jnp.sum(own.reshape(tok_rows, 2, owners, held * capacity), axis=1)
    rows_in = jnp.concatenate(
        [
            jnp.einsum(
                "top,td->opd",
                choose,
                tokens[:, q * piece:(q + 1) * piece],
                preferred_element_type=jnp.float32,
            ).astype(jnp.bfloat16)
            for q in range(pieces)
        ],
        axis=1,
    )

    known = lax.all_gather(
        jnp.concatenate([routes, gate_fixed], axis=1), "expert", axis=0, tiled=True
    )
    group_place = places(known[:, :2].reshape(owners, -1), experts, capacity)
    gates = known[:, 2:].astype(jnp.float32) / 65536.0
    cot = cotangent.astype(jnp.float32)
    gated = (gates[:, :, None] * cot[:, None, :]).astype(jnp.bfloat16)
    cot_in = jnp.einsum(
        "bap,bad->bpd",
        group_place,
        gated.reshape(owners, tok_rows * 2, breadth),
        preferred_element_type=jnp.float32,
    ).astype(jnp.bfloat16)
    cot_in = cot_in.reshape(owners, owners, held, capacity, breadth).transpose(1, 2, 0, 3, 4)
    cot_in = cot_in.reshape(owners, held, height, breadth)

    arrived, grad_rows = dispatch(rows_in, cot_in, owners, groups)

    sources = jnp.arange(span * pieces * held * capacity)
    slots = sources % capacity
    expert_of = sources // capacity % held
    piece_of = sources // (capacity * held) % pieces
    block_of = sources // (capacity * held * pieces)
    target = block_of * capacity + slots
    pick = (
        (expert_of == jnp.arange(held)[:, None, None, None])
        & (piece_of == jnp.arange(pieces)[:, None, None])
        & (target == jnp.arange(span * capacity)[:, None])
    ).astype(jnp.bfloat16)

    scale = (4.0 / threshold.astype(jnp.float32)).reshape(held, 1, hidden)
    wide_up = jnp.repeat(up_mask.astype(jnp.bfloat16), BLOCK, axis=2)
    wide_down = jnp.repeat(down_mask.astype(jnp.bfloat16), BLOCK, axis=2)
    wide_down = wide_down.reshape(held, tiles, tile // BLOCK, width)
    down_specs = [
        pl.BlockSpec((1, tile, width), lambda e, t: (e, t, 0)),
        pl.BlockSpec((1, 1, tile // BLOCK, width), lambda e, t: (e, t, 0, 0)),
    ]
    part, slope = pl.pallas_call(
        functools.partial(forward_kernel, span),
        grid=(held, tiles),
        out_shape=(
            jax.ShapeDtypeStruct((held, all_rows, width), jnp.bfloat16),
            jax.ShapeDtypeStruct((held, all_rows, hidden), jnp.bfloat16),
        ),
        in_specs=[
            pl.BlockSpec(arrived.shape, lambda e, t: (0, 0, 0)),
            pl.BlockSpec((1,) + pick.shape[1:], lambda e, t: (e, 0, 0, 0)),
            pl.BlockSpec((1, width, tile), lambda e, t: (e, 0, t)),
            pl.BlockSpec((1, width // BLOCK, tile), lambda e, t: (e, 0, t)),
            *down_specs,
            pl.BlockSpec((1, 1, tile), lambda e, t: (e, 0, t)),
        ],
        out_specs=(
            pl.BlockSpec((1, all_rows, width), lambda e, t: (e, 0, 0)),
            pl.BlockSpec((1, all_rows, tile), lambda e, t: (e, 0, t)),
        ),
        scratch_shapes=[
            pltpu.VMEM((all_rows, width), jnp.bfloat16),
            pltpu.VMEM((all_rows, width), jnp.float32),
        ],
        compiler_params=pltpu.CompilerParams(vmem_limit_bytes=VMEM_LIMIT),
        name="forward",
    )(arrived, pick, up_weight, wide_up, down_weight, wide_down, scale)

    ret = reduce_return(part.reshape(held, groups, height, width), owners)

    potential_grad = pl.pallas_call(
        backward_kernel,
        grid=(held, tiles),
        out_shape=jax.ShapeDtypeStruct((all_rows, held * hidden), jnp.bfloat16),
        in_specs=[
            pl.BlockSpec((1, all_rows, width), lambda e, t: (e, 0, 0)),
            *down_specs,
            pl.BlockSpec((1, all_rows, tile), lambda e, t: (e, 0, t)),
        ],
        out_specs=pl.BlockSpec((all_rows, tile), lambda e, t: (0, e * tiles + t)),
        compiler_params=pltpu.CompilerParams(vmem_limit_bytes=VMEM_LIMIT),
        name="backward",
    )(grad_rows, down_weight, wide_down, slope).reshape(all_rows, held, hidden)

    by_block = ret.reshape(owners, held, owners, capacity, breadth).transpose(2, 0, 1, 3, 4)
    picked = jnp.einsum(
        "bap,bpd->bad",
        group_place,
        by_block.reshape(owners, experts * capacity, breadth),
        preferred_element_type=jnp.float32,
    ).reshape(owners * tok_rows, 2, breadth)
    mixed = jnp.sum(gates[:, :, None] * picked, axis=1).astype(jnp.bfloat16)
    gate_part = jnp.sum(cot[:, None, :] * picked, axis=2)
    gate_grad = lax.psum_scatter(gate_part, "expert", scatter_dimension=0, tiled=True)
    return (mixed, gate_grad * (1.0 / math.sqrt(width)), potential_grad)


def solution(mesh):
    placed = (
        P(("dp", "expert"), None),
        P(("dp", "expert"), None),
        P(("dp", "expert"), None),
        P("expert", None, "dp"),
        P("expert", None, "dp"),
        P("expert", "dp", None),
        P("expert", "dp", None),
        P("expert", "dp"),
        P("dp", "expert"),
    )
    return jax.shard_map(
        shards,
        mesh=mesh,
        in_specs=placed,
        out_specs=(P("dp", "expert"), P(("dp", "expert"), None), P(None, "expert", "dp")),
        check_vma=False,
    )
```

time: 552 us -> 323 us (0.59)
  waiting for transfers between devices: 265 us -> 27.3 us
  Pallas kernels: 0 us -> 208 us
  local copies, waits for them, and re-layouts: 124 us -> 26.2 us
  matrix products: 63.5 us -> 7.27 us
  starting transfers between devices: 18.7 us -> 0.04 us
  other arithmetic: 26.8 us -> 10.9 us
  blocking collectives: 36.6 us -> 27.8 us
    pallas_call x0 -> x4, Pallas kernels: none -> 208 us  [the longest x1 68.9 us: dispatch(): pl.pallas_call(functools.partial(dispatch_kernel, owners, groups), out_sh...]
    all_to_all x4 -> x0, waiting for transfers between devices: 168 us -> none  [the longest x1 110 us: shards(): lax.all_to_all(cot_copies, ('dp', 'expert'), split_axis=0, concat_axis=0,...]
    unnamed x2 -> x1, waiting for transfers between devices: 97.5 us -> 0.02 us
    dot_general x3 -> x6, matrix products: 63.5 us -> 7.27 us  [the longest x2 3.45 us: shards(): jnp.einsum('top,td->opd', choose, tokens[:, q * piece:(q + 1) * piece], p...]
    unnamed x26 -> x12, local copies, waits for them, and re-layouts: 38.7 us -> 1.45 us
    all_to_all x1 -> x0, blocking collectives: 36.6 us -> none  [shards(): lax.all_to_all(summed.reshape(owners, capacity, local_experts, width), 'e...]
    convert_element_type x6 -> x5, local copies, waits for them, and re-layouts: 37.2 us -> 1.04 us  [the longest x1 0.74 us: shards(): cot_in = jnp.einsum('bap,bad->bpd', group_place, gated.reshape(owners, to...]
    all_gather x0 -> x1, blocking collectives: none -> 27.8 us  [shards(): lax.all_gather(jnp.concatenate([routes, gate_fixed], axis=1), 'expert', a...]
  transfers between devices with their start and end apart: 5 -> 1, of which waited for: 4 -> 1; matrix products, arithmetic and copies ran while one was open for 23% -> 5% of each run, Pallas kernels for 0% -> 6%
where the time goes in v1:
time: 323 us; the launch traced here: 322 us
  Pallas kernels  208 us (64%)
  blocking collectives  27.8 us (9%)
  waiting for transfers between devices  27.3 us (8%)
  local copies, waits for them, and re-layouts  26.2 us (8%)
  between operations  14.3 us (4%)
  other arithmetic  10.9 us (3%)
  matrix products  7.27 us (2%)
    pallas_call x1, Pallas kernels, dispatch(): pl.pallas_call(functools.partial(dispatch_kernel, owners, groups), out_sh...  68.9 us
    pallas_call x1, Pallas kernels, shards(): pl.pallas_call(functools.partial(forward_kernel, span), grid=(held, tiles...  60.8 us
    pallas_call x1, Pallas kernels, reduce_return(): pl.pallas_call(functools.partial(return_kernel, owners, groups, halves),...  58.3 us
    all_gather x1, blocking collectives, shards(): lax.all_gather(jnp.concatenate([routes, gate_fixed], axis=1), 'expert', a...  27.8 us
    reduce_scatter x1, waiting for transfers between devices, shards(): lax.psum_scatter(gate_part, 'expert', scatter_dimension=0, tiled=True)  27.3 us
    pallas_call x1, Pallas kernels, shards(): pl.pallas_call(backward_kernel, grid=(held, tiles), out_shape=jax.ShapeDt...  20 us
    reshape x1, local copies, waits for them, and re-layouts, shards(): potential_grad = pl.pallas_call(backward_kernel, grid=(held, tiles), out_...  7.09 us
  transfers between devices with their start and end apart: 1, of which 1 were waited for; matrix products, arithmetic and copies ran while one was open for 5% of the time, Pallas kernels for 6%

profile of v1, /device:TPU:0, one launch (start us, length us, event | category | flops | bytes accessed | tf_op | source)
XLA Modules:
  0.0 321.8 jit_solution(14989178611474674728)
XLA Ops:
  8.0 27.8 %all_gather.3 = s32[1024,4]{0,1:T(4,128)S(1)} all-gather(s32[128,4]{0,1:T(4,128)S(1)} %pad_add_fusion), channel_id=1, replica_groups=mesh['dp'=4,'expert'=8] {'expert'}, dimensions={0}, use_global_device_ids=true | all-gather | bytes 18432 | tf_op jit(solution)/shard_map/all_gather | solution.py:418
  35.8 0.8 copy.51
  38.0 1.3 convolution_convert_fusion
  39.3 2.2 convolution_convert_fusion.1
  43.3 0.7 reshape.288.m_up
  45.3 1.9 mul.84
  47.1 2.7 mul.85
  49.8 0.7 fusion.2
  51.3 0.7 copy.55
  52.1 1.4 copy.56.cot_in
  53.5 0.7 and_convert_fusion.pick
  54.2 1.2 pad_maximum_fusion.rows_in
  55.4 68.9 %dispatch.1 = (bf16[32,80,1024]{2,1,0:T(8,128)(2,1)}, bf16[2,640,2048]{2,1,0:T(8,128)(2,1)}) custom-call(bf16[8,80,1024]{2,1,0:T(8,128)(2,1)} %pad_maximum_fusion.rows_in, bf16[8,2,160,256]{3,2,1,0:T(8,128)(2,1)} %copy.56.cot_in), custom_call_target="tpu_custom_call" | custom-call | tf_op jit(solution)/shard_map/dispatch/pallas_call | solution.py:154
  124.4 60.8 %forward.1 = (bf16[2,640,2048]{2,1,0:T(8,128)(2,1)}, bf16[2,640,1792]{2,1,0:T(8,128)(2,1)}) custom-call(bf16[32,80,1024]{2,1,0:T(8,128)(2,1)} %get-tuple-element.7.arrived, bf16[2,2,80,320]{3,2,1,0:T(8,128)(2,1)} %and_convert_fusion.pick, bf16[2,2048,1792]{2,1,0:T(8,128)(2,1)} %w_up.1, bf16[2,16,1792]{2,1,0:T(8,128)(2,1)} %reshape.288.m_up, ...), custom_call_target="tpu_custom_call" | custom-call | tf_op jit(solution)/shard_map/forward/pallas_call | solution.py:456
  185.1 58.3 %reduce_return.1 = bf16[8,2,160,256]{3,2,1,0:T(8,128)(2,1)} custom-call(bf16[2,4,160,2048]{3,2,1,0:T(8,128)(2,1)} %bitcast.36), custom_call_target="tpu_custom_call" | custom-call | tf_op jit(solution)/shard_map/reduce_return/pallas_call | solution.py:287
  243.5 2.0 copy.59
  246.3 2.6 multiply_reduce_fusion
  248.8 1.3 reduce_sum.55
  250.1 2.5 reshape.293
  252.6 6.4 %multiply_reduce_fusion.1 = bf16[1024,256]{1,0:T(8,128)(2,1)} fusion(f32[1024,2,256]{2,1,0:T(2,128)S(1)} %reshape.293, f32[1024,2]{1,0:T(8,128)S(1)} %copy.49), kind=kLoop, calls=%fused_computation.4 | loop fusion | flops 786432 | bytes 2629632 | tf_op jit(solution)/shard_map/reduce_sum | solution.py:506
  259.1 20.0 %backward.1 = bf16[640,3584]{1,0:T(8,128)(2,1)} custom-call(bf16[2,640,2048]{2,1,0:T(8,128)(2,1)} %get-tuple-element.9.grad, bf16[2,1792,2048]{2,1,0:T(8,128)(2,1)} %w_down.3, bf16[2,7,2,2048]{3,2,1,0:T(2,128)(2,1)} %reshape_reshape.3.m_down, bf16[2,640,1792]{2,1,0:T(8,128)(2,1)} %get-tuple-element.10.slope), custom_call_target="tpu_custom_call" | custom-call | tf_op jit(solution)/shard_map/backward/pallas_call | solution.py:485
  279.1 7.1 %reshape.294 = bf16[640,2,1792]{2,1,0:T(2,128)(2,1)} reshape(bf16[640,3584]{1,0:T(8,128)(2,1)} %backward.1) | data formatting | bytes 9175040 | tf_op jit(solution)/shard_map/reshape | solution.py:497
  286.2 27.3 %reduce-scatter.2.cloned.1.call-done = f32[128,2]{1,0:T(8,128)} async-done(((f32[1024,2]{1,0:T(8,128)}), f32[128,2]{1,0:T(8,128)}) %reduce-scatter.2.cloned.1.call-update) | async-done | bytes 1040 | tf_op jit(solution)/shard_map/reduce_scatter | solution.py:508
  313.4 0.8 broadcast_multiply_fusion
  (47 shorter events, 7.3 us)
Async XLA Ops:
  7.2 34.4 %copy-start.3 = (s32[2,16,14]{1,0,2:T(2,128)S(1)}, s32[2,16,14]{1,0,2:T(2,128)}, u32[]{:S(2)}) copy-start(s32[2,16,14]{1,0,2:T(2,128)} %param.13) | copy-start | bytes 5380
  7.2 34.5 %copy-start.4 = (s32[2,14,16]{2,0,1:T(2,128)S(1)}, s32[2,14,16]{2,0,1:T(2,128)}, u32[]{:S(2)}) copy-start(s32[2,14,16]{2,0,1:T(2,128)} %param.15) | copy-start | bytes 5380
  7.2 34.5 %copy-start.2 = (s32[2,1792]{1,0:T(2,128)S(1)}, s32[2,1792]{1,0:T(2,128)}, u32[]{:S(2)}) copy-start(s32[2,1792]{1,0:T(2,128)} %param.16) | copy-start | bytes 43012
  7.2 306.2 %reduce-scatter.2.cloned.1.call-start = ((), (), s32[]{:S(2)}) async-start(), calls=%async_computation.1 | async-start | bytes 589824 | tf_op jit(solution)/shard_map/reduce_scatter | solution.py:508
  39.3 5.9 %copy-start.1 = (bf16[1024,256]{1,0:T(8,128)(2,1)S(1)}, bf16[1024,256]{1,0:T(8,128)(2,1)}, u32[]{:S(2)}) copy-start(bf16[1024,256]{1,0:T(8,128)(2,1)} %param.17) | copy-start | bytes 1572868
  52.1 2.1 copy-start
Sparse Core Ops, SparseCore 0:
  250.3 63.1 reduce-scatter.1

commit v2 on v1

--- a/solution.py
+++ b/solution.py
@@ -38,7 +38,8 @@
 
 
 def dispatch_kernel(
-    owners, groups, rows_in, cot_in, rows_out, cot_out, local, first, twin, across, landed
+    owners, groups, span, tile, rows_in, cot_in, pick, w_up, m_up, w_down, m_down, scale,
+    cot_out, part, slope, rows_out, rows, total, local, first, twin, across, landed
 ):
     me, mine = lax.axis_index("dp"), lax.axis_index("expert")
     turns = groups // CORES
@@ -117,29 +118,72 @@
             cross(kind, d, source).start()
         relay(kind, 0, source).start()
 
-    for kind in (0, 1):
-        keep(kind).wait()
-        pass_on(kind, mine)
-
-        def own(k):
-            source = lax.rem(mine + owners - k, owners)
-            arrival(kind, me, source).wait_recv()
-            pass_on(kind, source)
-
-        over(1, own)
-        for d in range(1, turns):
-            group = lax.rem(x + turns - d, turns) * CORES + core
-
-            def far(k):
-                source = lax.rem(mine + owners - k, owners)
-                arrival(kind, group, source).wait_recv()
-                relay(kind, d, source).start()
-
-            over(0, far)
-    for kind in (0, 1):
+    def own(kind, k):
+        source = lax.rem(mine + owners - k, owners)
+        arrival(kind, me, source).wait_recv()
+        pass_on(kind, source)
+
+    def far(kind, d, k):
+        group = lax.rem(x + turns - d, turns) * CORES + core
+        source = lax.rem(mine + owners - k, owners)
+        arrival(kind, group, source).wait_recv()
+        relay(kind, d, source).start()
+
+    def last(kind):
         for d in range(turns):
             group = lax.rem(x + turns - d, turns) * CORES + 1 - core
             over(0, lambda k: arrival(kind, group, k).wait_recv())
+
+    keep(0).wait()
+    pass_on(0, mine)
+    over(1, lambda k: own(0, k))
+    for d in range(1, turns):
+        over(0, lambda k: far(0, d, k))
+    last(0)
+    keep(1).wait()
+    pass_on(1, mine)
+
+    held, _, hidden = w_up.shape
+    tiles = hidden // tile
+    steps = held * tiles
+
+    def body(pick, w_up, m_up, w_down, m_down, scale, part, slope):
+        step = pl.program_id(0) * tiles + pl.program_id(1)
+
+        @pl.when((step >= 1) & (step < owners))
+        def _():
+            own(1, step)
+
+        forward_step(
+            pl.program_id(1), tiles, span, rows_out, pick, w_up, m_up, w_down, m_down, scale,
+            part, slope, rows, total,
+        )
+
+    width = w_up.shape[1]
+    all_rows = rows.shape[0]
+    pltpu.emit_pipeline(
+        body,
+        grid=(held, tiles),
+        in_specs=[
+            pl.BlockSpec((1,) + pick.shape[1:], lambda e, t: (e, 0, 0, 0)),
+            pl.BlockSpec((1, width, tile), lambda e, t: (e, 0, t)),
+            pl.BlockSpec((1, width // BLOCK, tile), lambda e, t: (e, 0, t)),
+            pl.BlockSpec((1, tile, width), lambda e, t: (e, t, 0)),
+            pl.BlockSpec((1, 1, tile // BLOCK, width), lambda e, t: (e, t, 0, 0)),
+            pl.BlockSpec((1, 1, tile), lambda e, t: (e, 0, t)),
+        ],
+        out_specs=[
+            pl.BlockSpec((1, all_rows, width), lambda e, t: (e, 0, 0)),
+            pl.BlockSpec((1, all_rows, tile), lambda e, t: (e, 0, t)),
+        ],
+    )(pick, w_up, m_up, w_down, m_down, scale, part, slope)
+
+    if steps < owners:
+        lax.fori_loop(steps, owners, lambda k, c: (own(1, k), c)[1], 0)
+    for d in range(1, turns):
+        over(0, lambda k: far(1, d, k))
+    last(1)
+    for kind in (0, 1):
         over(1, lambda k: send_first(kind, k).wait_send())
         for d in range(turns):
             over(0, lambda k: relay(kind, d, k).wait_send())
@@ -147,19 +191,25 @@
             over(0, lambda k: cross(kind, d, k).wait_send())
 
 
-def dispatch(rows_in, cot_in, owners, groups):
+def dispatch(rows_in, cot_in, pick, w_up, m_up, w_down, m_down, scale, owners, groups, span, tile):
     _, packed, piece = rows_in.shape
     _, experts, height, breadth = cot_in.shape
     turns = groups // CORES
+    hidden = w_up.shape[2]
+    all_rows, width = groups * height, owners * breadth
     return pl.pallas_call(
-        functools.partial(dispatch_kernel, owners, groups),
+        functools.partial(dispatch_kernel, owners, groups, span, tile),
         out_shape=(
-            jax.ShapeDtypeStruct((groups * owners, packed, piece), jnp.bfloat16),
-            jax.ShapeDtypeStruct((experts, groups * height, owners * breadth), jnp.bfloat16),
+            jax.ShapeDtypeStruct((experts, all_rows, width), jnp.bfloat16),
+            jax.ShapeDtypeStruct((experts, all_rows, width), jnp.bfloat16),
+            jax.ShapeDtypeStruct((experts, all_rows, hidden), jnp.bfloat16),
         ),
-        in_specs=[pl.BlockSpec(memory_space=pl.ANY)] * 2,
-        out_specs=(pl.BlockSpec(memory_space=pl.ANY),) * 2,
+        in_specs=[pl.BlockSpec(memory_space=pl.ANY)] * 8,
+        out_specs=(pl.BlockSpec(memory_space=pl.ANY),) * 3,
         scratch_shapes=[
+            pltpu.VMEM((groups * owners, packed, piece), jnp.bfloat16),
+            pltpu.VMEM((all_rows, width), jnp.bfloat16),
+            pltpu.VMEM((all_rows, width), jnp.float32),
             pltpu.SemaphoreType.DMA((2,)),
             pltpu.SemaphoreType.DMA((2, owners)),
             pltpu.SemaphoreType.DMA((2, turns, owners)),
@@ -170,11 +220,11 @@
             collective_id=0, has_side_effects=True, vmem_limit_bytes=VMEM_LIMIT
         ),
         name="dispatch",
-    )(rows_in, cot_in)
+    )(rows_in, cot_in, pick, w_up, m_up, w_down, m_down, scale)
 
 
 def return_kernel(
-    owners, groups, halves, part, ret, near, sums, far, done,
+    owners, groups, halves, tile, part, grad, w_down, m_down, slope, ret, out, near, sums, far, done,
     near_s, near_r, far_s, far_r, back_s, back_r, local
 ):
     me, mine = lax.axis_index("dp"), lax.axis_index("expert")
@@ -251,7 +301,7 @@
     for e, h in chunks:
         for d in order:
             fold(e, h, d).start()
-    for e, h in chunks:
+    def pair(e, h):
         for d in order:
             fold(e, h, d).wait_recv()
             group = lax.rem(x + d, turns) * CORES + core
@@ -261,7 +311,8 @@
             ).astype(jnp.bfloat16)
             if d > 0:
                 cross(e, h, d).start()
-    for e, h in chunks:
+
+    def finish(e, h):
         total = sums[e, 0, band(h)].astype(jnp.float32)
         for d in range(1, turns):
             cross(e, h, d).wait_recv()
@@ -269,6 +320,37 @@
         done[e, band(h)] = total.astype(jnp.bfloat16)
         over(lambda k: give(e, h, k).start())
         keep(e, h).start()
+
+    hidden = slope.shape[2]
+    tiles = hidden // tile
+    steps = experts * tiles
+    duties = [(i, functools.partial(pair, *c)) for i, c in enumerate(chunks)]
+    duties += [
+        (min(steps - 1, 6 + 4 * i), functools.partial(finish, *c)) for i, c in enumerate(chunks)
+    ]
+    inside = [duty for duty in duties if duty[0] < steps - 1]
+    after = [duty for duty in duties if duty[0] >= steps - 1]
+
+    def body(grad, w_down, m_down, slope, out):
+        step = pl.program_id(0) * tiles + pl.program_id(1)
+        for at, act in inside:
+            pl.when(step == at)(act)
+        backward_kernel(grad, w_down, m_down, slope, out)
+
+    all_rows = grad.shape[1]
+    pltpu.emit_pipeline(
+        body,
+        grid=(experts, tiles),
+        in_specs=[
+            pl.BlockSpec((1, all_rows, width), lambda e, t: (e, 0, 0)),
+            pl.BlockSpec((1, tile, width), lambda e, t: (e, t, 0)),
+            pl.BlockSpec((1, 1, tile // BLOCK, width), lambda e, t: (e, t, 0, 0)),
+            pl.BlockSpec((1, all_rows, tile), lambda e, t: (e, 0, t)),
+        ],
+        out_specs=[pl.BlockSpec((all_rows, tile), lambda e, t: (0, e * tiles + t))],
+    )(grad, w_down, m_down, slope, out)
+    for _, act in after:
+        act()
     for e, h in chunks:
         keep(e, h).wait()
         over(lambda k: arrival(e, h, lax.rem(mine + k, owners)).wait_recv())
@@ -279,16 +361,19 @@
             cross(e, h, d).wait_send()
 
 
-def reduce_return(part, owners):
+def reduce_return(part, grad, w_down, m_down, slope, owners, tile):
     experts, groups, height, width = part.shape
     turns = groups // CORES
     halves = 2 if height % 32 == 0 else 1
     sems = pltpu.SemaphoreType.DMA
     return pl.pallas_call(
-        functools.partial(return_kernel, owners, groups, halves),
-        out_shape=jax.ShapeDtypeStruct((owners, experts, height, width // owners), jnp.bfloat16),
-        in_specs=[pl.BlockSpec(memory_space=pltpu.VMEM)],
-        out_specs=pl.BlockSpec(memory_space=pl.ANY),
+        functools.partial(return_kernel, owners, groups, halves, tile),
+        out_shape=(
+            jax.ShapeDtypeStruct((owners, experts, height, width // owners), jnp.bfloat16),
+            jax.ShapeDtypeStruct((slope.shape[1], experts * slope.shape[2]), jnp.bfloat16),
+        ),
+        in_specs=[pl.BlockSpec(memory_space=pltpu.VMEM)] + [pl.BlockSpec(memory_space=pl.ANY)] * 4,
+        out_specs=(pl.BlockSpec(memory_space=pl.ANY),) * 2,
         scratch_shapes=[
             pltpu.VMEM((experts, turns, height, width), jnp.bfloat16),
             pltpu.VMEM((experts, turns, height, width), jnp.bfloat16),
@@ -306,17 +391,70 @@
             collective_id=1, has_side_effects=True, vmem_limit_bytes=VMEM_LIMIT
         ),
         name="reduce_return",
-    )(part)
+    )(part, grad, w_down, m_down, slope)
+
+
+def swap_kernel(owners, give_all, mine_in, out, send, recv):
+    me, mine = lax.axis_index("dp"), lax.axis_index("expert")
+    barrier = pltpu.get_barrier_semaphore()
+
+    def hail(k, carry):
+        peer = lax.rem(mine + k, owners)
+        pl.semaphore_signal(
+            barrier, inc=1, device_id={"dp": me, "expert": peer}, device_id_type=MESH
+        )
+        return carry
+
+    def copy(k, source, peer):
+        return pltpu.make_async_remote_copy(
+            src_ref=mine_in if give_all else mine_in.at[peer],
+            dst_ref=out.at[source],
+            send_sem=send.at[k],
+            recv_sem=recv.at[source],
+            device_id={"dp": me, "expert": peer},
+            device_id_type=MESH,
+        )
+
+    def begin(k, carry):
+        copy(k, mine, lax.rem(mine + k, owners)).start()
+        return carry
+
+    def end(k, carry):
+        peer = lax.rem(mine + k, owners)
+        copy(k, peer, peer).wait_recv()
+        copy(k, mine, peer).wait_send()
+        return carry
+
+    lax.fori_loop(1, owners, hail, 0)
+    pl.semaphore_wait(barrier, owners - 1)
+    lax.fori_loop(1, owners, begin, 0)
+    out[mine] = mine_in[...] if give_all else mine_in[mine]
+    lax.fori_loop(1, owners, end, 0)
+
+
+def swap(values, owners, give_all, number):
+    shape = values.shape if give_all else values.shape[1:]
+    return pl.pallas_call(
+        functools.partial(swap_kernel, owners, give_all),
+        out_shape=jax.ShapeDtypeStruct((owners,) + shape, values.dtype),
+        in_specs=[pl.BlockSpec(memory_space=pltpu.VMEM)],
+        out_specs=pl.BlockSpec(memory_space=pltpu.VMEM),
+        scratch_shapes=[
+            pltpu.SemaphoreType.DMA((owners,)),
+            pltpu.SemaphoreType.DMA((owners,)),
+        ],
+        compiler_params=pltpu.CompilerParams(collective_id=number, has_side_effects=True),
+        name="share" if give_all else "swap",
+    )(values)
 
 
 def masked(weights, mask):
     return (weights.reshape(mask.shape[0], BLOCK, -1) * mask[:, None, :]).reshape(weights.shape)
 
 
-def forward_kernel(
-    span, arrived, pick, w_up, m_up, w_down, m_down, scale, part, slope, rows, total
+def forward_step(
+    tile, tiles, span, arrived, pick, w_up, m_up, w_down, m_down, scale, part, slope, rows, total
 ):
-    tile, tiles = pl.program_id(1), pl.num_programs(1)
     pieces, out_rows = pick.shape[1], pick.shape[2]
     piece = arrived.shape[2]
 
@@ -415,9 +553,8 @@
         axis=1,
     )
 
-    known = lax.all_gather(
-        jnp.concatenate([routes, gate_fixed], axis=1), "expert", axis=0, tiled=True
-    )
+    known = swap(jnp.concatenate([routes, gate_fixed], axis=1).T, owners, True, 2)
+    known = known.transpose(0, 2, 1).reshape(owners * tok_rows, 4)
     group_place = places(known[:, :2].reshape(owners, -1), experts, capacity)
     gates = known[:, 2:].astype(jnp.float32) / 65536.0
     cot = cotangent.astype(jnp.float32)
@@ -431,8 +568,6 @@
     cot_in = cot_in.reshape(owners, owners, held, capacity, breadth).transpose(1, 2, 0, 3, 4)
     cot_in = cot_in.reshape(owners, held, height, breadth)
 
-    arrived, grad_rows = dispatch(rows_in, cot_in, owners, groups)
-
     sources = jnp.arange(span * pieces * held * capacity)
     slots = sources % capacity
     expert_of = sources // capacity % held
@@ -449,52 +584,15 @@
     wide_up = jnp.repeat(up_mask.astype(jnp.bfloat16), BLOCK, axis=2)
     wide_down = jnp.repeat(down_mask.astype(jnp.bfloat16), BLOCK, axis=2)
     wide_down = wide_down.reshape(held, tiles, tile // BLOCK, width)
-    down_specs = [
-        pl.BlockSpec((1, tile, width), lambda e, t: (e, t, 0)),
-        pl.BlockSpec((1, 1, tile // BLOCK, width), lambda e, t: (e, t, 0, 0)),
-    ]
-    part, slope = pl.pallas_call(
-        functools.partial(forward_kernel, span),
-        grid=(held, tiles),
-        out_shape=(
-            jax.ShapeDtypeStruct((held, all_rows, width), jnp.bfloat16),
-            jax.ShapeDtypeStruct((held, all_rows, hidden), jnp.bfloat16),
-        ),
-        in_specs=[
-            pl.BlockSpec(arrived.shape, lambda e, t: (0, 0, 0)),
-            pl.BlockSpec((1,) + pick.shape[1:], lambda e, t: (e, 0, 0, 0)),
-            pl.BlockSpec((1, width, tile), lambda e, t: (e, 0, t)),
-            pl.BlockSpec((1, width // BLOCK, tile), lambda e, t: (e, 0, t)),
-            *down_specs,
-            pl.BlockSpec((1, 1, tile), lambda e, t: (e, 0, t)),
-        ],
-        out_specs=(
-            pl.BlockSpec((1, all_rows, width), lambda e, t: (e, 0, 0)),
-            pl.BlockSpec((1, all_rows, tile), lambda e, t: (e, 0, t)),
-        ),
-        scratch_shapes=[
-            pltpu.VMEM((all_rows, width), jnp.bfloat16),
-            pltpu.VMEM((all_rows, width), jnp.float32),
-        ],
-        compiler_params=pltpu.CompilerParams(vmem_limit_bytes=VMEM_LIMIT),
-        name="forward",
-    )(arrived, pick, up_weight, wide_up, down_weight, wide_down, scale)
-
-    ret = reduce_return(part.reshape(held, groups, height, width), owners)
-
-    potential_grad = pl.pallas_call(
-        backward_kernel,
-        grid=(held, tiles),
-        out_shape=jax.ShapeDtypeStruct((all_rows, held * hidden), jnp.bfloat16),
-        in_specs=[
-            pl.BlockSpec((1, all_rows, width), lambda e, t: (e, 0, 0)),
-            *down_specs,
-            pl.BlockSpec((1, all_rows, tile), lambda e, t: (e, 0, t)),
-        ],
-        out_specs=pl.BlockSpec((all_rows, tile), lambda e, t: (0, e * tiles + t)),
-        compiler_params=pltpu.CompilerParams(vmem_limit_bytes=VMEM_LIMIT),
-        name="backward",
-    )(grad_rows, down_weight, wide_down, slope).reshape(all_rows, held, hidden)
+    grad_rows, part, slope = dispatch(
+        rows_in, cot_in, pick, up_weight, wide_up, down_weight, wide_down, scale,
+        owners, groups, span, tile,
+    )
+    ret, potential_grad = reduce_return(
+        part.reshape(held, groups, height, width),
+        grad_rows, down_weight, wide_down, slope, owners, tile,
+    )
+    potential_grad = potential_grad.reshape(all_rows, held, hidden)
 
     by_block = ret.reshape(owners, held, owners, capacity, breadth).transpose(2, 0, 1, 3, 4)
     picked = jnp.einsum(
@@ -505,7 +603,8 @@
     ).reshape(owners * tok_rows, 2, breadth)
     mixed = jnp.sum(gates[:, :, None] * picked, axis=1).astype(jnp.bfloat16)
     gate_part = jnp.sum(cot[:, None, :] * picked, axis=2)
-    gate_grad = lax.psum_scatter(gate_part, "expert", scatter_dimension=0, tiled=True)
+    gate_part = gate_part.reshape(owners, tok_rows, 2).transpose(0, 2, 1)
+    gate_grad = jnp.sum(swap(gate_part, owners, False, 3), axis=0).T
     return (mixed, gate_grad * (1.0 / math.sqrt(width)), potential_grad)
 
 

time: 323 us -> 233 us (0.72)
  blocking collectives: 27.8 us -> 0 us
  waiting for transfers between devices: 27.3 us -> 0 us
  Pallas kernels: 208 us -> 186 us
  between operations: 14.3 us -> 0.86 us
  other arithmetic: 10.9 us -> 14.8 us
    all_gather x1 -> x0, blocking collectives: 27.8 us -> none  [shards(): lax.all_gather(jnp.concatenate([routes, gate_fixed], axis=1), 'expert', a...]
    reduce_scatter x1 -> x0, waiting for transfers between devices: 27.3 us -> none  [shards(): lax.psum_scatter(gate_part, 'expert', scatter_dimension=0, tiled=True)]
    pallas_call x4, Pallas kernels: 208 us -> 186 us  [the longest x1 106 us: dispatch(): pl.pallas_call(functools.partial(dispatch_kernel, owners, groups, span, t...]
    reshape x1 -> x2, local copies, waits for them, and re-layouts: 7.09 us -> 7.76 us  [the longest x1 7.08 us: shards(): potential_grad = potential_grad.reshape(all_rows, held, hidden)]
  transfers between devices with their start and end apart: 1 -> 0, of which waited for: 1 -> 0; matrix products, arithmetic and copies ran while one was open for 5% -> 0% of each run, Pallas kernels for 6% -> 0%
where the time goes in v2:
time: 233 us; the launch traced here: 231 us
  Pallas kernels  186 us (80%)
  local copies, waits for them, and re-layouts  25.7 us (11%)
  other arithmetic  14.8 us (6%)
  matrix products  4.43 us (2%)
    pallas_call x1, Pallas kernels, dispatch(): pl.pallas_call(functools.partial(dispatch_kernel, owners, groups, span, t...  106 us
    pallas_call x1, Pallas kernels, reduce_return(): pl.pallas_call(functools.partial(return_kernel, owners, groups, halves, t...  60.5 us
    pallas_call x2, Pallas kernels, swap(): pl.pallas_call(functools.partial(swap_kernel, owners, give_all), out_shap...  18.6 us
    reshape x1, local copies, waits for them, and re-layouts, shards(): potential_grad = potential_grad.reshape(all_rows, held, hidden)  7.08 us
    reduce_sum x1, other arithmetic, shards(): mixed = jnp.sum(gates[:, :, None] * picked, axis=1).astype(jnp.bfloat16)  6.43 us

profile of v2, /device:TPU:0, one launch (start us, length us, event | category | flops | bytes accessed | tf_op | source)
XLA Modules:
  0.0 231.4 jit_solution(3559927078636569135)
XLA Ops:
  0.6 1.3 add_bitcast_fusion.mine_in
  2.1 0.7 convert_element_type.108
  3.6 9.7 %share.1 = s32[8,4,128]{2,1,0:T(4,128)} custom-call(s32[4,128]{1,0:T(4,128)} %add_bitcast_fusion.mine_in), custom_call_target="tpu_custom_call" | custom-call | tf_op jit(solution)/shard_map/share/pallas_call | solution.py:437
  14.0 0.7 fusion.24
  14.7 0.7 convert_divide_fusion
  16.1 0.8 copy.67
  19.3 0.8 reshape.296.m_up
  20.0 0.7 and_convert_fusion.pick
  22.7 1.2 pad_maximum_fusion.rows_in
  23.9 1.9 mul.87
  25.8 2.7 %mul.88 = f32[8,256,256]{2,1,0:T(8,128)S(1)} reshape(f32[1024,2,256]{2,1,0:T(2,128)} %mul.87) | data formatting | bytes 4194304 | tf_op jit(solution)/shard_map/mul | solution.py:561
  28.5 0.7 fusion.2
  29.2 0.7 copy.70
  30.0 0.7 copy.71
  30.7 1.3 copy.74.cot_in
  32.1 106.5 %dispatch.1 = (bf16[2,640,2048]{2,1,0:T(8,128)(2,1)}, bf16[2,640,2048]{2,1,0:T(8,128)(2,1)}, bf16[2,640,1792]{2,1,0:T(8,128)(2,1)}) custom-call(bf16[8,80,1024]{2,1,0:T(8,128)(2,1)} %pad_maximum_fusion.rows_in, bf16[8,2,160,256]{3,2,1,0:T(8,128)(2,1)} %copy.74.cot_in, bf16[2,2,80,320]{3,2,1,0:T(8,128)(2,1)} %and_convert_fusion.pick, ...), custom_call_target="tpu_custom_call" | custom-call | tf_op jit(solution)/shard_map/dispatch/pallas_call | solution.py:200
  138.5 60.5 %reduce_return.1 = (bf16[8,2,160,256]{3,2,1,0:T(8,128)(2,1)}, bf16[640,3584]{1,0:T(8,128)(2,1)}) custom-call(bf16[2,4,160,2048]{3,2,1,0:T(8,128)(2,1)} %bitcast.49, bf16[2,640,2048]{2,1,0:T(8,128)(2,1)} %get-tuple-element.9.grad, bf16[2,1792,2048]{2,1,0:T(8,128)(2,1)} %w_down.3, bf16[2,7,2,2048]{3,2,1,0:T(2,128)(2,1)} %reshape_reshape.3.m_down, ...), custom_call_target="tpu_custom_call" | custom-call | tf_op jit(solution)/shard_map/reduce_return/pallas_call | solution.py:369
  199.0 2.0 copy.75
  201.1 0.7 copy.76
  201.8 2.5 %multiply_reduce_fusion = (f32[8,256]{1,0:T(8,128)S(1)}, f32[8,256,256]{2,1,0:T(8,128)}) fusion(f32[8,256,256]{2,1,0:T(8,128)S(1)} %mul.88, bf16[8,320,256]{2,0,1:T(8,128)(2,1)S(1)} %bitcast.48, s32[8,256]{1,0:T(8,128)S(1)} %convert_add_fusion), kind=kOutput, calls=%fused_computation.3 | convolution fusion | flops 337246208 | bytes 5521408 | tf_op jit(solution)/shard_map/bap,bpd->bad/dot_general | solution.py:598
  205.1 8.9 %swap.1 = f32[8,2,128]{2,1,0:T(2,128)} custom-call(f32[8,2,128]{2,1,0:T(2,128)} %bitcast.53), custom_call_target="tpu_custom_call" | custom-call | tf_op jit(solution)/shard_map/swap/pallas_call | solution.py:437
  215.4 2.5 %reshape.301 = f32[1024,2,256]{2,1,0:T(2,128)S(1)} reshape(f32[8,256,256]{2,1,0:T(8,128)} %get-tuple-element.14) | data formatting | bytes 4194304 | tf_op jit(solution)/shard_map/reshape | solution.py:603
  217.9 6.4 %multiply_reduce_fusion.1 = bf16[1024,256]{1,0:T(8,128)(2,1)} fusion(f32[1024,2,256]{2,1,0:T(2,128)S(1)} %reshape.301, f32[1024,2]{1,0:T(8,128)S(1)} %copy.65), kind=kLoop, calls=%fused_computation.4 | loop fusion | flops 786432 | bytes 2629632 | tf_op jit(solution)/shard_map/reduce_sum | solution.py:604
  224.3 7.1 %reshape.303 = bf16[640,2,1792]{2,1,0:T(2,128)(2,1)} reshape(bf16[640,3584]{1,0:T(8,128)(2,1)} %get-tuple-element.12) | data formatting | bytes 9175040 | tf_op jit(solution)/shard_map/reshape | solution.py:595
  (38 shorter events, 8.6 us)
Async XLA Ops:
  0.6 21.4 %copy-start.1 = (bf16[128,2048]{1,0:T(8,128)(2,1)S(1)}, bf16[128,2048]{1,0:T(8,128)(2,1)}, u32[]{:S(2)}) copy-start(bf16[128,2048]{1,0:T(8,128)(2,1)} %param.9) | copy-start | bytes 1572868
  22.1 1.9 copy-start

commit v3 on v2

--- a/solution.py
+++ b/solution.py
@@ -3,6 +3,7 @@
 
 import jax
 import jax.numpy as jnp
+import numpy as np
 from jax import lax
 from jax.experimental import pallas as pl
 from jax.experimental.pallas import tpu as pltpu
@@ -39,7 +40,7 @@
 
 def dispatch_kernel(
     owners, groups, span, tile, rows_in, cot_in, pick, w_up, m_up, w_down, m_down, scale,
-    cot_out, part, slope, rows_out, rows, total, local, first, twin, across, landed
+    cot_out, part, slope, rows_out, rows, units, local, first, twin, across, landed
 ):
     me, mine = lax.axis_index("dp"), lax.axis_index("expert")
     turns = groups // CORES
@@ -134,54 +135,99 @@
             group = lax.rem(x + turns - d, turns) * CORES + 1 - core
             over(0, lambda k: arrival(kind, group, k).wait_recv())
 
+    held, width, hidden = w_up.shape
+    all_rows = rows.shape[1]
+    pieces, out_rows = pick.shape[0], pick.shape[1] // held
+    piece = rows_out.shape[2]
+    spans = owners // span
+
+    def unpack(group):
+        def step(i, carry):
+            at = group * spans + i
+            box = rows_out[pl.ds(at * span, span)].reshape(-1, piece)
+            top = pl.multiple_of(at * out_rows, 16)
+            for q in range(pieces):
+                got = jnp.dot(pick[q], box, preferred_element_type=jnp.float32)
+                for e in range(held):
+                    rows[e, pl.ds(top, out_rows), q * piece:(q + 1) * piece] = got[
+                        e * out_rows:(e + 1) * out_rows
+                    ].astype(jnp.bfloat16)
+            return carry
+
+        lax.fori_loop(0, spans, step, 0)
+
     keep(0).wait()
     pass_on(0, mine)
     over(1, lambda k: own(0, k))
+    unpack(me)
     for d in range(1, turns):
         over(0, lambda k: far(0, d, k))
-    last(0)
+    for d in range(1, turns):
+        unpack(lax.rem(x + turns - d, turns) * CORES + core)
+    for d in range(turns):
+        group = lax.rem(x + turns - d, turns) * CORES + 1 - core
+        over(0, lambda k: arrival(0, group, k).wait_recv())
+        unpack(group)
     keep(1).wait()
     pass_on(1, mine)
 
-    held, _, hidden = w_up.shape
     tiles = hidden // tile
     steps = held * tiles
 
-    def body(pick, w_up, m_up, w_down, m_down, scale, part, slope):
-        step = pl.program_id(0) * tiles + pl.program_id(1)
+    def up_body(w_up, m_up, scale, slope):
+        e, t = pl.program_id(0), pl.program_id(1)
+        step = e * tiles + t
 
         @pl.when((step >= 1) & (step < owners))
         def _():
             own(1, step)
 
-        forward_step(
-            pl.program_id(1), tiles, span, rows_out, pick, w_up, m_up, w_down, m_down, scale,
-            part, slope, rows, total,
-        )
-
-    width = w_up.shape[1]
-    all_rows = rows.shape[0]
+        up = masked(w_up[0], m_up[0])
+        potential = jnp.dot(rows[e], up, preferred_element_type=jnp.float32)
+        sig = jax.nn.sigmoid(potential)
+        scaled = sig * scale[0]
+        units[e, :, pl.ds(pl.multiple_of(t * tile, 128), tile)] = (potential * scaled).astype(
+            jnp.bfloat16
+        )
+        slope[0] = (scaled * (1.0 + potential * (1.0 - sig))).astype(jnp.bfloat16)
+
     pltpu.emit_pipeline(
-        body,
+        up_body,
         grid=(held, tiles),
         in_specs=[
-            pl.BlockSpec((1,) + pick.shape[1:], lambda e, t: (e, 0, 0, 0)),
             pl.BlockSpec((1, width, tile), lambda e, t: (e, 0, t)),
             pl.BlockSpec((1, width // BLOCK, tile), lambda e, t: (e, 0, t)),
-            pl.BlockSpec((1, tile, width), lambda e, t: (e, t, 0)),
-            pl.BlockSpec((1, 1, tile // BLOCK, width), lambda e, t: (e, t, 0, 0)),
             pl.BlockSpec((1, 1, tile), lambda e, t: (e, 0, t)),
         ],
-        out_specs=[
-            pl.BlockSpec((1, all_rows, width), lambda e, t: (e, 0, 0)),
-            pl.BlockSpec((1, all_rows, tile), lambda e, t: (e, 0, t)),
-        ],
-    )(pick, w_up, m_up, w_down, m_down, scale, part, slope)
-
+        out_specs=[pl.BlockSpec((1, all_rows, tile), lambda e, t: (e, 0, t))],
+    )(w_up, m_up, scale, slope)
     if steps < owners:
         lax.fori_loop(steps, owners, lambda k, c: (own(1, k), c)[1], 0)
+
+    wide = 512
+    strips = width // wide
+    relayed = min(owners, held * strips)
+
+    def down_body(w_down, m_down, part):
+        e = pl.program_id(0)
+        step = e * strips + pl.program_id(1)
+        if turns > 1:
+            pl.when(step < relayed)(lambda: far(1, 1, step))
+        down = masked(w_down[0], m_down[0])
+        part[0] = jnp.dot(units[e], down, preferred_element_type=jnp.float32).astype(jnp.bfloat16)
+
+    pltpu.emit_pipeline(
+        down_body,
+        grid=(held, strips),
+        in_specs=[
+            pl.BlockSpec((1, hidden, wide), lambda e, t: (e, 0, t)),
+            pl.BlockSpec((1, hidden // BLOCK, wide), lambda e, t: (e, 0, t)),
+        ],
+        out_specs=[pl.BlockSpec((1, all_rows, wide), lambda e, t: (e, 0, t))],
+    )(w_down, m_down, part)
+
     for d in range(1, turns):
-        over(0, lambda k: far(1, d, k))
+        over(relayed if d == 1 else 0, lambda k: far(1, d, k))
     last(1)
     for kind in (0, 1):
         over(1, lambda k: send_first(kind, k).wait_send())
@@ -204,12 +250,14 @@
             jax.ShapeDtypeStruct((experts, all_rows, width), jnp.bfloat16),
             jax.ShapeDtypeStruct((experts, all_rows, hidden), jnp.bfloat16),
         ),
-        in_specs=[pl.BlockSpec(memory_space=pl.ANY)] * 8,
+        in_specs=[pl.BlockSpec(memory_space=pl.ANY)] * 2
+        + [pl.BlockSpec(memory_space=pltpu.VMEM)]
+        + [pl.BlockSpec(memory_space=pl.ANY)] * 5,
         out_specs=(pl.BlockSpec(memory_space=pl.ANY),) * 3,
         scratch_shapes=[
             pltpu.VMEM((groups * owners, packed, piece), jnp.bfloat16),
-            pltpu.VMEM((all_rows, width), jnp.bfloat16),
-            pltpu.VMEM((all_rows, width), jnp.float32),
+            pltpu.VMEM((experts, all_rows, width), jnp.bfloat16),
+            pltpu.VMEM((experts, all_rows, hidden), jnp.bfloat16),
             pltpu.SemaphoreType.DMA((2,)),
             pltpu.SemaphoreType.DMA((2, owners)),
             pltpu.SemaphoreType.DMA((2, turns, owners)),
@@ -452,46 +500,6 @@
     return (weights.reshape(mask.shape[0], BLOCK, -1) * mask[:, None, :]).reshape(weights.shape)
 
 
-def forward_step(
-    tile, tiles, span, arrived, pick, w_up, m_up, w_down, m_down, scale, part, slope, rows, total
-):
-    pieces, out_rows = pick.shape[1], pick.shape[2]
-    piece = arrived.shape[2]
-
-    @pl.when(tile == 0)
-    def _():
-        def unpack(g, carry):
-            box = arrived[pl.ds(g * span, span)].reshape(-1, piece)
-            for q in range(pieces):
-                rows[pl.ds(pl.multiple_of(g * out_rows, 16), out_rows), q * piece:(q + 1) * piece] = jnp.dot(
-                    pick[0, q], box, preferred_element_type=jnp.float32
-                ).astype(jnp.bfloat16)
-            return carry
-
-        lax.fori_loop(0, arrived.shape[0] // span, unpack, 0)
-
-    up = masked(w_up[0], m_up[0])
-    potential = jnp.dot(rows[...], up, preferred_element_type=jnp.float32)
-    sig = jax.nn.sigmoid(potential)
-    scaled = sig * scale[0]
-    hidden = (potential * scaled).astype(jnp.bfloat16)
-    slope[0] = (scaled * (1.0 + potential * (1.0 - sig))).astype(jnp.bfloat16)
-    down = masked(w_down[0], m_down[0, 0])
-    term = jnp.dot(hidden, down, preferred_element_type=jnp.float32)
-
-    @pl.when(tile == 0)
-    def _():
-        total[...] = term
-
-    @pl.when(tile > 0)
-    def _():
-        total[...] += term
-
-    @pl.when(tile == tiles - 1)
-    def _():
-        part[0] = total[...].astype(jnp.bfloat16)
-
-
 def backward_kernel(grad, w_down, m_down, slope, out):
     down = masked(w_down[0], m_down[0, 0])
     back = lax.dot_general(
@@ -501,18 +509,25 @@
 
 
 def places(routes, experts, capacity):
-    onehot = (routes[..., None] == jnp.arange(experts, dtype=jnp.int32)).astype(jnp.bfloat16)
-    count = routes.shape[1]
-    at = jnp.arange(count)
+    names = jnp.arange(experts, dtype=jnp.int32)
+    first, second = [(r[..., None] == names).astype(jnp.bfloat16) for r in routes]
+    at = jnp.arange(first.shape[1])
     earlier = jnp.einsum(
         "ab,nbe->nae",
         (at[:, None] > at[None, :]).astype(jnp.bfloat16),
-        onehot,
+        first + second,
         preferred_element_type=jnp.float32,
     )
-    slot = jnp.sum(earlier * onehot.astype(jnp.float32), axis=-1).astype(jnp.int32)
-    place = routes * capacity + slot
-    return (place[..., None] == jnp.arange(experts * capacity, dtype=jnp.int32)).astype(jnp.bfloat16)
+    spots = jnp.arange(experts * capacity, dtype=jnp.int32)
+
+    def mark(route, onehot, before):
+        slot = jnp.sum(before * onehot.astype(jnp.float32), axis=-1).astype(jnp.int32)
+        return ((route * capacity + slot)[..., None] == spots).astype(jnp.bfloat16)
+
+    return (
+        mark(routes[0], first, earlier),
+        mark(routes[1], second, earlier + first.astype(jnp.float32)),
+    )
 
 
 def shards(
@@ -538,8 +553,9 @@
     tile = 256 if hidden % 256 == 0 else BLOCK
     tiles = hidden // tile
 
-    own = places(routes.reshape(1, -1), experts, capacity)[0]
-    choose = jnp.sum(own.reshape(tok_rows, 2, owners, held * capacity), axis=1)
+    table = jnp.concatenate([routes, gate_fixed], axis=1).T
+    own = places((table[None, 0], table[None, 1]), experts, capacity)
+    choose = (own[0] + own[1]).reshape(tok_rows, owners, held * capacity)
     rows_in = jnp.concatenate(
         [
             jnp.einsum(
@@ -553,57 +569,56 @@
         axis=1,
     )
 
-    known = swap(jnp.concatenate([routes, gate_fixed], axis=1).T, owners, True, 2)
-    known = known.transpose(0, 2, 1).reshape(owners * tok_rows, 4)
-    group_place = places(known[:, :2].reshape(owners, -1), experts, capacity)
-    gates = known[:, 2:].astype(jnp.float32) / 65536.0
-    cot = cotangent.astype(jnp.float32)
-    gated = (gates[:, :, None] * cot[:, None, :]).astype(jnp.bfloat16)
-    cot_in = jnp.einsum(
-        "bap,bad->bpd",
-        group_place,
-        gated.reshape(owners, tok_rows * 2, breadth),
-        preferred_element_type=jnp.float32,
+    known = swap(table, owners, True, 2)
+    marks = places((known[:, 0], known[:, 1]), experts, capacity)
+    gates = [known[:, 2 + k].astype(jnp.float32)[..., None] / 65536.0 for k in range(2)]
+    cot = cotangent.reshape(owners, tok_rows, breadth).astype(jnp.float32)
+    cot_in = sum(
+        jnp.einsum(
+            "btp,btd->bpd",
+            mark,
+            (gate * cot).astype(jnp.bfloat16),
+            preferred_element_type=jnp.float32,
+        )
+        for mark, gate in zip(marks, gates)
     ).astype(jnp.bfloat16)
     cot_in = cot_in.reshape(owners, owners, held, capacity, breadth).transpose(1, 2, 0, 3, 4)
     cot_in = cot_in.reshape(owners, held, height, breadth)
 
-    sources = jnp.arange(span * pieces * held * capacity)
-    slots = sources % capacity
+    sources = np.arange(span * pieces * held * capacity)
     expert_of = sources // capacity % held
     piece_of = sources // (capacity * held) % pieces
     block_of = sources // (capacity * held * pieces)
-    target = block_of * capacity + slots
-    pick = (
-        (expert_of == jnp.arange(held)[:, None, None, None])
-        & (piece_of == jnp.arange(pieces)[:, None, None])
-        & (target == jnp.arange(span * capacity)[:, None])
-    ).astype(jnp.bfloat16)
+    target = (expert_of * span + block_of) * capacity + sources % capacity
+    pick = jnp.asarray(
+        (piece_of == np.arange(pieces)[:, None, None])
+        & (target == np.arange(held * span * capacity)[:, None]),
+        jnp.bfloat16,
+    )
 
     scale = (4.0 / threshold.astype(jnp.float32)).reshape(held, 1, hidden)
     wide_up = jnp.repeat(up_mask.astype(jnp.bfloat16), BLOCK, axis=2)
     wide_down = jnp.repeat(down_mask.astype(jnp.bfloat16), BLOCK, axis=2)
-    wide_down = wide_down.reshape(held, tiles, tile // BLOCK, width)
     grad_rows, part, slope = dispatch(
         rows_in, cot_in, pick, up_weight, wide_up, down_weight, wide_down, scale,
         owners, groups, span, tile,
     )
     ret, potential_grad = reduce_return(
         part.reshape(held, groups, height, width),
-        grad_rows, down_weight, wide_down, slope, owners, tile,
+        grad_rows, down_weight, wide_down.reshape(held, tiles, tile // BLOCK, width),
+        slope, owners, tile,
     )
     potential_grad = potential_grad.reshape(all_rows, held, hidden)
 
     by_block = ret.reshape(owners, held, owners, capacity, breadth).transpose(2, 0, 1, 3, 4)
-    picked = jnp.einsum(
-        "bap,bpd->bad",
-        group_place,
-        by_block.reshape(owners, experts * capacity, breadth),
-        preferred_element_type=jnp.float32,
-    ).reshape(owners * tok_rows, 2, breadth)
-    mixed = jnp.sum(gates[:, :, None] * picked, axis=1).astype(jnp.bfloat16)
-    gate_part = jnp.sum(cot[:, None, :] * picked, axis=2)
-    gate_part = gate_part.reshape(owners, tok_rows, 2).transpose(0, 2, 1)
+    by_block = by_block.reshape(owners, experts * capacity, breadth)
+    picked = [
+        jnp.einsum("btp,bpd->btd", mark, by_block, preferred_element_type=jnp.float32)
+        for mark in marks
+    ]
+    mixed = (gates[0] * picked[0] + gates[1] * picked[1]).astype(jnp.bfloat16)
+    mixed = mixed.reshape(owners * tok_rows, breadth)
+    gate_part = jnp.stack([jnp.sum(cot * p, axis=2) for p in picked], axis=1)
     gate_grad = jnp.sum(swap(gate_part, owners, False, 3), axis=0).T
     return (mixed, gate_grad * (1.0 / math.sqrt(width)), potential_grad)
 

time: 233 us -> 191 us (0.82)
  Pallas kernels: 186 us -> 160 us
  local copies, waits for them, and re-layouts: 25.7 us -> 16.7 us
  other arithmetic: 14.8 us -> 6.83 us
    pallas_call x1, Pallas kernels: 106 us -> 82.9 us  [dispatch(): pl.pallas_call(functools.partial(dispatch_kernel, owners, groups, span, t...]
    reduce_sum x2 -> x0, other arithmetic: 6.54 us -> none  [the longest x1 6.43 us: shards(): mixed = jnp.sum(gates[:, :, None] * picked, axis=1).astype(jnp.bfloat16)]
    mul x3 -> x0, local copies, waits for them, and re-layouts: 4.82 us -> none  [the longest x2 4.55 us: shards(): gated = (gates[:, :, None] * cot[:, None, :]).astype(jnp.bfloat16)]
    reshape x3 -> x2, local copies, waits for them, and re-layouts: 3.44 us -> 0.72 us  [shards(): wide_down = jnp.repeat(down_mask.astype(jnp.bfloat16), BLOCK, axis=2)]
where the time goes in v3:
time: 191 us; the launch traced here: 189 us
  Pallas kernels  160 us (84%)
  local copies, waits for them, and re-layouts  16.7 us (9%)
  other arithmetic  6.83 us (4%)
  matrix products  5.3 us (3%)
    pallas_call x1, Pallas kernels, dispatch(): pl.pallas_call(functools.partial(dispatch_kernel, owners, groups, span, t...  82.9 us
    pallas_call x1, Pallas kernels, reduce_return(): pl.pallas_call(functools.partial(return_kernel, owners, groups, halves, t...  58.2 us
    pallas_call x2, Pallas kernels, swap(): pl.pallas_call(functools.partial(swap_kernel, owners, give_all), out_shap...  18.6 us
    reshape x1, local copies, waits for them, and re-layouts, shards(): potential_grad = potential_grad.reshape(all_rows, held, hidden)  7.08 us

profile of v3, /device:TPU:0, one launch (start us, length us, event | category | flops | bytes accessed | tf_op | source)
XLA Modules:
  0.0 189.3 jit_solution(18038111900844468774)
XLA Ops:
  0.6 0.8 add_bitcast_fusion.mine_in
  1.7 0.7 convert_element_type.200
  2.5 0.7 convert_element_type.201
  3.3 9.7 %share.1 = s32[8,4,128]{2,1,0:T(4,128)} custom-call(s32[4,128]{1,0:T(4,128)} %copy-done.2), custom_call_target="tpu_custom_call" | custom-call | tf_op jit(solution)/shard_map/share/pallas_call | solution.py:485
  12.9 0.8 fusion.55
  13.7 0.8 convert_multiply_fusion.6
  14.7 0.7 convert_divide_fusion
  16.3 0.7 copy.29.m_down
  17.0 0.7 copy.23.m_down
  17.8 0.8 reshape.231.m_up
  19.4 1.2 pad_maximum_fusion.rows_in
  21.8 0.7 copy.19
  22.5 0.7 copy.20
  23.2 1.3 copy.22.cot_in
  24.6 82.9 %dispatch.1 = (bf16[2,640,2048]{2,1,0:T(8,128)(2,1)}, bf16[2,640,2048]{2,1,0:T(8,128)(2,1)}, bf16[2,640,1792]{2,1,0:T(8,128)(2,1)}) custom-call(bf16[8,80,1024]{2,1,0:T(8,128)(2,1)} %pad_maximum_fusion.rows_in, bf16[8,2,160,256]{3,2,1,0:T(8,128)(2,1)} %copy.22.cot_in, bf16[2,160,320]{2,1,0:T(8,128)(2,1)} %constant.18.clone.pick, ...), custom_call_target="tpu_custom_call" | custom-call | tf_op jit(solution)/shard_map/dispatch/pallas_call | solution.py:246
  107.5 58.2 %reduce_return.1 = (bf16[8,2,160,256]{3,2,1,0:T(8,128)(2,1)}, bf16[640,3584]{1,0:T(8,128)(2,1)}) custom-call(bf16[2,4,160,2048]{3,2,1,0:T(8,128)(2,1)} %bitcast.70, bf16[2,640,2048]{2,1,0:T(8,128)(2,1)} %get-tuple-element.9.grad, bf16[2,1792,2048]{2,1,0:T(8,128)(2,1)} %w_down.3, bf16[2,7,2,2048]{3,2,1,0:T(2,128)(2,1)} %copy.29.m_down, ...), custom_call_target="tpu_custom_call" | custom-call | tf_op jit(solution)/shard_map/reduce_return/pallas_call | solution.py:417
  165.7 2.0 %copy.25 = bf16[8,2,160,256]{3,0,2,1:T(8,128)(2,1)S(1)} copy(bf16[8,2,160,256]{3,2,1,0:T(8,128)(2,1)} %get-tuple-element.11) | data formatting | bytes 2621440 | tf_op jit(solution)/shard_map/reduce_return/pallas_call | solution.py:417
  167.8 0.7 copy.26
  168.5 0.7 fusion
  169.2 2.2 %fusion.7 = (f32[8,128]{1,0:T(8,128)S(1)}, f32[8,128]{1,0:T(8,128)S(1)}, bf16[8,128,256]{2,1,0:T(8,128)(2,1)}) fusion(bf16[8,128,256]{2,1,0:T(8,128)(2,1)S(1)} %bitcast.73, f32[8,128,256]{2,1,0:T(8,128)S(1)} %fusion, f32[8,128]{1,0:T(8,128)S(1)} %bitcast.81, f32[8,128]{1,0:T(8,128)S(1)} %bitcast.75, bf16[8,320,256]{2,0,1:T(8,128)(2,1)S(1)} %bitcast.66, ...), kind=kOutput, calls=%fused_computation.19 | convolution fusion | flops 170457088 | bytes 3428352 | tf_op jit(solution)/shard_map/btp,bpd->btd/dot_general | solution.py:616
  171.4 0.6 pad_maximum_fusion.1.mine_in
  172.0 9.0 %swap.1 = f32[8,2,128]{2,1,0:T(2,128)} custom-call(f32[8,2,128]{2,1,0:T(2,128)} %pad_maximum_fusion.1.mine_in), custom_call_target="tpu_custom_call" | custom-call | tf_op jit(solution)/shard_map/swap/pallas_call | solution.py:485
  181.0 0.7 reduce_sum.69
  182.3 7.1 %reshape.238 = bf16[640,2,1792]{2,1,0:T(2,128)(2,1)} reshape(bf16[640,3584]{1,0:T(8,128)(2,1)} %get-tuple-element.12) | data formatting | bytes 9175040 | tf_op jit(solution)/shard_map/reshape | solution.py:611
  (23 shorter events, 4.0 us)
Async XLA Ops:
  0.6 18.0 %copy-start.1 = (bf16[128,2048]{1,0:T(8,128)(2,1)S(1)}, bf16[128,2048]{1,0:T(8,128)(2,1)}, u32[]{:S(2)}) copy-start(bf16[128,2048]{1,0:T(8,128)(2,1)} %param.10) | copy-start | bytes 1572868
  1.4 1.8 copy-start.2
  19.4 1.2 copy-start

commit v4 on v3

--- a/solution.py
+++ b/solution.py
@@ -372,9 +372,9 @@
     hidden = slope.shape[2]
     tiles = hidden // tile
     steps = experts * tiles
-    duties = [(i, functools.partial(pair, *c)) for i, c in enumerate(chunks)]
+    duties = [(i // 2, functools.partial(pair, *c)) for i, c in enumerate(chunks)]
     duties += [
-        (min(steps - 1, 6 + 4 * i), functools.partial(finish, *c)) for i, c in enumerate(chunks)
+        (min(steps - 1, 3 + i), functools.partial(finish, *c)) for i, c in enumerate(chunks)
     ]
     inside = [duty for duty in duties if duty[0] < steps - 1]
     after = [duty for duty in duties if duty[0] >= steps - 1]
@@ -412,7 +412,7 @@
 def reduce_return(part, grad, w_down, m_down, slope, owners, tile):
     experts, groups, height, width = part.shape
     turns = groups // CORES
-    halves = 2 if height % 32 == 0 else 1
+    halves = height // 32 if height % 32 == 0 else 1
     sems = pltpu.SemaphoreType.DMA
     return pl.pallas_call(
         functools.partial(return_kernel, owners, groups, halves, tile),

time: 191 us -> 189 us (0.990)
  Pallas kernels: 160 us -> 158 us
where the time goes in v4:
time: 189 us; the launch traced here: 187 us
  Pallas kernels  158 us (84%)
  local copies, waits for them, and re-layouts  16.7 us (9%)
  other arithmetic  6.83 us (4%)
  matrix products  5.3 us (3%)
    pallas_call x1, Pallas kernels, dispatch(): pl.pallas_call(functools.partial(dispatch_kernel, owners, groups, span, t...  82.9 us
    pallas_call x1, Pallas kernels, reduce_return(): pl.pallas_call(functools.partial(return_kernel, owners, groups, halves, t...  57.4 us
    pallas_call x2, Pallas kernels, swap(): pl.pallas_call(functools.partial(swap_kernel, owners, give_all), out_shap...  17.4 us
    reshape x1, local copies, waits for them, and re-layouts, shards(): potential_grad = potential_grad.reshape(all_rows, held, hidden)  7.08 us

profile of v4, /device:TPU:0, one launch (start us, length us, event | category | flops | bytes accessed | tf_op | source)
XLA Modules:
  0.0 187.3 jit_solution(9435599016006876994)
XLA Ops:
  0.6 0.8 add_bitcast_fusion.mine_in
  1.7 0.7 convert_element_type.200
  2.5 0.7 convert_element_type.201
  3.3 9.7 %share.1 = s32[8,4,128]{2,1,0:T(4,128)} custom-call(s32[4,128]{1,0:T(4,128)} %copy-done.2), custom_call_target="tpu_custom_call" | custom-call | tf_op jit(solution)/shard_map/share/pallas_call | solution.py:485
  12.9 0.8 fusion.55
  13.7 0.8 convert_multiply_fusion.6
  14.7 0.7 convert_divide_fusion
  16.3 0.7 copy.29.m_down
  17.0 0.7 copy.23.m_down
  17.8 0.8 reshape.231.m_up
  19.4 1.2 pad_maximum_fusion.rows_in
  21.8 0.7 copy.19
  22.5 0.7 copy.20
  23.2 1.3 copy.22.cot_in
  24.6 82.9 %dispatch.1 = (bf16[2,640,2048]{2,1,0:T(8,128)(2,1)}, bf16[2,640,2048]{2,1,0:T(8,128)(2,1)}, bf16[2,640,1792]{2,1,0:T(8,128)(2,1)}) custom-call(bf16[8,80,1024]{2,1,0:T(8,128)(2,1)} %pad_maximum_fusion.rows_in, bf16[8,2,160,256]{3,2,1,0:T(8,128)(2,1)} %copy.22.cot_in, bf16[2,160,320]{2,1,0:T(8,128)(2,1)} %constant.18.clone.pick, ...), custom_call_target="tpu_custom_call" | custom-call | tf_op jit(solution)/shard_map/dispatch/pallas_call | solution.py:246
  107.5 57.4 %reduce_return.1 = (bf16[8,2,160,256]{3,2,1,0:T(8,128)(2,1)}, bf16[640,3584]{1,0:T(8,128)(2,1)}) custom-call(bf16[2,4,160,2048]{3,2,1,0:T(8,128)(2,1)} %bitcast.70, bf16[2,640,2048]{2,1,0:T(8,128)(2,1)} %get-tuple-element.9.grad, bf16[2,1792,2048]{2,1,0:T(8,128)(2,1)} %w_down.3, bf16[2,7,2,2048]{3,2,1,0:T(2,128)(2,1)} %copy.29.m_down, ...), custom_call_target="tpu_custom_call" | custom-call | tf_op jit(solution)/shard_map/reduce_return/pallas_call | solution.py:417
  164.9 2.0 %copy.25 = bf16[8,2,160,256]{3,0,2,1:T(8,128)(2,1)S(1)} copy(bf16[8,2,160,256]{3,2,1,0:T(8,128)(2,1)} %get-tuple-element.11) | data formatting | bytes 2621440 | tf_op jit(solution)/shard_map/reduce_return/pallas_call | solution.py:417
  167.0 0.7 copy.26
  167.7 0.7 fusion
  168.4 2.2 %fusion.7 = (f32[8,128]{1,0:T(8,128)S(1)}, f32[8,128]{1,0:T(8,128)S(1)}, bf16[8,128,256]{2,1,0:T(8,128)(2,1)}) fusion(bf16[8,128,256]{2,1,0:T(8,128)(2,1)S(1)} %bitcast.73, f32[8,128,256]{2,1,0:T(8,128)S(1)} %fusion, f32[8,128]{1,0:T(8,128)S(1)} %bitcast.81, f32[8,128]{1,0:T(8,128)S(1)} %bitcast.75, bf16[8,320,256]{2,0,1:T(8,128)(2,1)S(1)} %bitcast.66, ...), kind=kOutput, calls=%fused_computation.19 | convolution fusion | flops 170457088 | bytes 3428352 | tf_op jit(solution)/shard_map/btp,bpd->btd/dot_general | solution.py:616
  170.6 0.6 pad_maximum_fusion.1.mine_in
  171.2 7.7 %swap.1 = f32[8,2,128]{2,1,0:T(2,128)} custom-call(f32[8,2,128]{2,1,0:T(2,128)} %pad_maximum_fusion.1.mine_in), custom_call_target="tpu_custom_call" | custom-call | tf_op jit(solution)/shard_map/swap/pallas_call | solution.py:485
  179.0 0.7 reduce_sum.69
  180.2 7.1 %reshape.238 = bf16[640,2,1792]{2,1,0:T(2,128)(2,1)} reshape(bf16[640,3584]{1,0:T(8,128)(2,1)} %get-tuple-element.12) | data formatting | bytes 9175040 | tf_op jit(solution)/shard_map/reshape | solution.py:611
  (23 shorter events, 4.0 us)
Async XLA Ops:
  0.6 18.0 %copy-start.1 = (bf16[128,2048]{1,0:T(8,128)(2,1)S(1)}, bf16[128,2048]{1,0:T(8,128)(2,1)}, u32[]{:S(2)}) copy-start(bf16[128,2048]{1,0:T(8,128)(2,1)} %param.10) | copy-start | bytes 1572868
  1.4 1.8 copy-start.2
  19.4 1.2 copy-start
